TPU v7x, 32 devices: a whole 2x2x4 slice. The times are simulated.
32 devices in a mesh: dp: 8 (over z, y), tensor: 4 (over x, core).
Axes of the slice: x: 2, y: 2, z: 4, core: 2. Of those that a mesh axis runs over, the one named last changes fastest.
Arguments:
- hidden: bfloat16 [16, 1024, 2048], P('dp', 'tensor'), may hold values from -6 to 6
- pre_gain: float32 [2048], replicated, may hold values from 0.5 to 1.5
- w_zx: bfloat16 [2, 2048, 4096], P(None, 'dp', 'tensor'), may hold values from -0.125 to 0.125
- w_bcdt: bfloat16 [2048, 320], P('dp'), may hold values from -0.125 to 0.125
- conv_x: float32 [5, 4096], P(None, 'tensor'), may hold values from -0.5 to 0.5
- conv_bc: float32 [5, 256], replicated, may hold values from -0.5 to 0.5
- dt_bias: float32 [64], P('tensor'), may hold values from -6 to -2
- a_log: float32 [64], P('tensor'), may hold values from 0 to 2.5
- d_skip: float32 [64], P('tensor'), may hold values from 0.5 to 1.5
- gate_gain: float32 [4096], P('tensor'), may hold values from 0.5 to 1.5
- w_out: bfloat16 [4096, 2048], P('tensor', 'dp'), may hold values from -0.09375 to 0.09375
- cotangent: bfloat16 [16, 1024, 2048], P('dp', 'tensor'), may hold values from -6 to 6
- segments: int32 [16, 1024], P('dp'), may hold values from 0 to 1023, as said below
Outputs:
- out_hidden: bfloat16 [16, 1024, 2048], P('dp', 'tensor')
- d_hidden: float32 [16, 1024, 2048], P('dp', 'tensor')
- d_pre_gain: float32 [2048], replicated
- d_w_zx: float32 [2, 2048, 4096], P(None, 'dp', 'tensor')
- d_w_bcdt: float32 [2048, 320], P('dp')
- d_conv_x: float32 [5, 4096], P(None, 'tensor')
- d_conv_bc: float32 [5, 256], replicated
- d_dt_bias: float32 [64], P('tensor')
- d_a_log: float32 [64], P('tensor')
- d_d_skip: float32 [64], P('tensor')
- d_gate_gain: float32 [4096], P('tensor')
- d_w_out: float32 [4096, 2048], P('tensor', 'dp')
Inputs may be any that keep to these rules, and one draw needn't show every extreme that they name: `segments`: within each sequence a document is numbered by the position of its first token, so numbers never fall along a sequence and the first token has 0; every sequence's last token begins a document of its own, and in every sequence one document covers the positions from 255 to 768.
All inputs are finite; a program needn't handle non-finite values.
Results may differ from a plain program's by a relative error of at most 0.009.
Values may be sent and summed in bfloat16 or wider, within the bound.
A program may use at most 320 MiB of HBM per device.

v0:
```python
import functools

import jax
import jax.numpy as jnp
import numpy as np
from jax import lax
from jax.experimental import pallas as pl
from jax.experimental.pallas import tpu as pltpu
from jax.sharding import PartitionSpec as P

MESH = pl.DeviceIdType.MESH
EPS = 1e-05
BLOCK = 256
F32 = jnp.float32
BF16 = jnp.bfloat16
EXACT = lax.Precision.HIGHEST
LOG2E = 1.4426950408889634
NEG = -1e30


def sigmoid(v):
    return 0.5 * jnp.tanh(0.5 * v) + 0.5


def split3(v):
    hi = v.astype(BF16)
    rest = v - hi.astype(F32)
    mid = rest.astype(BF16)
    low = (rest - mid.astype(F32)).astype(BF16)
    return hi, mid, low


def dot(a, b):
    return jnp.dot(a, b, preferred_element_type=F32)


def dot_nt(a, b):
    return lax.dot_general(a, b, (((1,), (1,)), ((), ())), preferred_element_type=F32)


def dot_tn(a, b):
    return lax.dot_general(a, b, (((0,), (0,)), ((), ())), preferred_element_type=F32)


def softplus(v):
    return jnp.maximum(v, 0.0) + jnp.log1p(jnp.exp(-jnp.abs(v)))


def head_rows(raw, dt_bias, a_log):
    q = raw.shape[1]
    upto = (
        lax.broadcasted_iota(jnp.int32, (q, q), 0) <= lax.broadcasted_iota(jnp.int32, (q, q), 1)
    ).astype(F32)
    biased = raw + dt_bias
    step = softplus(biased)
    rate = -jnp.exp(a_log) * step
    cum = jnp.dot(rate, upto, precision=EXACT, preferred_element_type=F32) * LOG2E
    return biased, step, rate, cum


def exact_nt(a, b):
    a_hi, a_mid, _ = split3(a)
    b_hi, b_mid, _ = split3(b)
    return dot_nt(a_hi, b_hi) + dot_nt(a_hi, b_mid) + dot_nt(a_mid, b_hi)


def turned(row):
    k = row.shape[1]
    own = lax.broadcasted_iota(jnp.int32, (k, k), 0) == lax.broadcasted_iota(jnp.int32, (k, k), 1)
    return jnp.sum(jnp.where(own, row, 0.0), axis=1, keepdims=True)


def to_columns(rows):
    return jnp.concatenate([rows, jnp.zeros((128 - rows.shape[0], rows.shape[1]), F32)], axis=0).T


def head_columns(reads, last, step, cum, third):
    cum_end = cum[:, BLOCK - 1 : BLOCK]
    rows = []
    for factor in (reads * jnp.exp2(cum), last * jnp.exp2(cum_end - cum) * step):
        hi, mid, _ = split3(factor)
        rows += [hi.astype(F32), mid.astype(F32)]
    cols = to_columns(jnp.concatenate(rows + [third], axis=0))
    return cols[:, 4 * cum.shape[0] :], cols.astype(BF16), jnp.exp2(cum_end)


def log2_step(step):
    return jnp.log(jnp.maximum(step, 1e-37)) * LOG2E


def forward_block(
    block, x, bc, dt, marks_ref, taps_x_ref, taps_bc_ref, bias_ref, alog_ref, skip_ref, spread_ref, pick_ref,
    y_ref, cx_ref, cbc_ref, states_ref,
    xs, bs, state, mask_bias,
):
    q = BLOCK
    heads = dt.shape[0]
    channels = x.shape[-1]
    width = channels // heads

    @pl.when(block == 0)
    def _():
        xs[0:8, :] = jnp.zeros((8, xs.shape[1]), F32)
        bs[0:8, :] = jnp.zeros((8, bs.shape[1]), F32)
        state[...] = jnp.zeros_like(state)

    marks = to_columns(marks_ref[0])
    lag_masks = [marks[:, k : k + 1] for k in range(3)]

    def conv(hold, at, taps_ref):
        out = taps_ref[4:5, at] + taps_ref[3:4, at] * hold[8 : 8 + q, at]
        for lag in (1, 2, 3):
            out = out + (lag_masks[lag - 1] * hold[8 - lag : 8 - lag + q, at]) * taps_ref[3 - lag : 4 - lag, at]
        return out

    bs[8 : 8 + q, :] = bc
    xs[8 : 8 + q, :] = x
    cbc = conv(bs, slice(None), taps_bc_ref)
    cbc_ref[0] = cbc
    bc = cbc * sigmoid(cbc)
    n = bc.shape[1] // 2
    scores = exact_nt(bc[:, n:], bc[:, :n])
    b_mat, c_mat = bc[:, :n].astype(BF16), bc[:, n:].astype(BF16)
    b_turned = b_mat.T

    _, step, _, cum = head_rows(dt, turned(bias_ref[...]), turned(alog_ref[...]))
    cols, factors, carry = head_columns(marks_ref[0, 3:4, :], marks_ref[0, 4:5, :], step, cum, cum)
    source = cum - log2_step(step)
    carry_e = jnp.sum(carry * spread_ref[...].astype(F32), axis=0, keepdims=True)

    rows = lax.broadcasted_iota(jnp.int32, (q, q), 0)
    places = lax.broadcasted_iota(jnp.int32, (q, q), 1)
    mask_bias[...] = jnp.where((marks[:, 5:6] == marks_ref[0, 5:6, :]) & (rows >= places), 0.0, NEG)

    half = q // 2
    pair_width = 2 * width
    lane = lax.broadcasted_iota(jnp.int32, (1, pair_width), 1)
    every = slice(0, channels)
    cx = conv(xs, every, taps_x_ref)
    cx_ref[0] = cx
    xb = (cx * sigmoid(cx)).astype(BF16)
    xf = xb.astype(F32)
    stb = state[...].astype(BF16)
    states_ref[0, 0] = stb
    y_ref[...] = dot(c_mat, stb) * dot(factors, pick_ref[:, :channels]) + skip_ref[...] * xf
    scaled = (xf * dot(factors, pick_ref[:, channels:])).astype(BF16)
    state[...] = carry_e * state[...] + dot(b_turned, scaled)
    for pair in range(heads // 2):
        at = slice(pair * pair_width, (pair + 1) * pair_width)
        xp = xb[:, at]
        tops, lows = [], []
        for h in (2 * pair, 2 * pair + 1):
            col = cols[:, h : h + 1]
            row = source[h : h + 1, :]
            top = jnp.exp2((col[:half] - row[:, :half]) + mask_bias[:half, :half]) * scores[:half, :half]
            low = jnp.exp2((col[half:] - row) + mask_bias[half:, :]) * scores[half:, :]
            tops.append(top.astype(BF16))
            lows.append(low.astype(BF16))
        top = dot(jnp.concatenate(tops, axis=0), xp[:half])
        low = dot(jnp.concatenate(lows, axis=0), xp)
        first = lane < width
        y_ref[:half, at] += jnp.where(first, top[:half], top[half:])
        y_ref[half:, at] += jnp.where(first, low[:half], low[half:])

    xs[0:8, :] = xs[q : q + 8, :]
    bs[0:8, :] = bs[q : q + 8, :]


def backward_block(
    seq, step_id, dy_ref, x_ref, cx_ref, bc_ref, cbc_ref, dt_ref, marks_ref, states_ref,
    taps_x_ref, taps_bc_ref, bias_ref, alog_ref, skip_ref, spread_ref, pick_ref,
    dx_ref, dbc_ref, gx_ref, gbc_ref, gh_ref,
    ds_x, ds_bc, d_state, mask_bias, d_scores, d_in, row_sums,
):
    q = BLOCK
    heads = dt_ref.shape[1]
    channels = x_ref.shape[-1]
    width = channels // heads

    @pl.when(step_id == 0)
    def _():
        ds_x[:, q : q + 8, :] = jnp.zeros((3, 8, channels), F32)
        ds_bc[:, q : q + 8, :] = jnp.zeros((3, 8, ds_bc.shape[2]), F32)
        d_state[...] = jnp.zeros_like(d_state)

    @pl.when((step_id == 0) & (seq == 0))
    def _():
        gx_ref[...] = jnp.zeros_like(gx_ref)
        gbc_ref[...] = jnp.zeros_like(gbc_ref)
        gh_ref[...] = jnp.zeros_like(gh_ref)

    marks = to_columns(marks_ref[0])
    lag_masks = [marks[:, k : k + 1] for k in range(3)]

    def conv_back(d_out, value, hold, at, taps_ref, grad_ref):
        value = value.astype(F32)
        d_value = d_out * taps_ref[3:4, at]
        grad_ref[3:4, at] += jnp.sum(value * d_out, axis=0, keepdims=True)
        grad_ref[4:5, at] += jnp.sum(d_out, axis=0, keepdims=True)
        for lag in (1, 2, 3):
            hold[lag - 1, 0:q, at] = lag_masks[lag - 1] * d_out
            moved = hold[lag - 1, lag : lag + q, at]
            d_value = d_value + moved * taps_ref[3 - lag : 4 - lag, at]
            grad_ref[3 - lag : 4 - lag, at] += jnp.sum(value * moved, axis=0, keepdims=True)
            hold[lag - 1, q : q + 8, at] = hold[lag - 1, 0:8, at]
        return d_value

    cbc = cbc_ref[0]
    bc = cbc * sigmoid(cbc)
    n = bc.shape[1] // 2
    scores = exact_nt(bc[:, :n], bc[:, n:])
    b_mat, c_mat = bc[:, :n].astype(BF16), bc[:, n:].astype(BF16)
    c_turned = c_mat.T

    a_log = turned(alog_ref[...])
    biased, step, rate, cum = head_rows(dt_ref[0], turned(bias_ref[...]), a_log)
    source = cum - log2_step(step)
    cols, factors, carry = head_columns(marks_ref[0, 3:4, :], marks_ref[0, 4:5, :], step, cum, source)
    carry_e = jnp.sum(carry * spread_ref[...].astype(F32), axis=0, keepdims=True)

    rows = lax.broadcasted_iota(jnp.int32, (q, q), 0)
    places = lax.broadcasted_iota(jnp.int32, (q, q), 1)
    mask_bias[...] = jnp.where((marks[:, 5:6] == marks_ref[0, 5:6, :]) & (rows <= places), 0.0, NEG)

    half = q // 2
    pair_width = 2 * width
    lane = lax.broadcasted_iota(jnp.int32, (1, pair_width), 1)
    first = lane < width
    d_scores[...] = jnp.zeros_like(d_scores)
    col_h = jnp.zeros((heads, q), F32)
    head_row = lax.broadcasted_iota(jnp.int32, (heads, 3 * half), 0)
    spread = spread_ref[...]
    cx = cx_ref[0]
    xb = (cx * sigmoid(cx)).astype(BF16)
    dyb = dy_ref[0]
    st = states_ref[0, 0]
    dye = dyb.astype(F32) * dot(factors, pick_ref[:, :channels])
    out_h = dot_nt(spread, (dye * dot(c_mat, st)).astype(BF16))
    dye = dye.astype(BF16)
    d_c = dot_nt(dye, st)
    dst = d_state[...].astype(BF16)
    kept = jnp.sum(d_state[...] * st.astype(F32), axis=0, keepdims=True) * carry_e
    carried = jnp.sum(spread.astype(F32) * kept, axis=1, keepdims=True)
    d_state[...] = carry_e * d_state[...] + dot(c_turned, dye)
    xf = xb.astype(F32)
    to_end = dot(factors, pick_ref[:, channels:])
    d_b = dot_nt((xf * to_end).astype(BF16), dst)
    dx_st = dot(b_mat, dst) * to_end
    state_h = dot_nt(spread, (xf * dx_st).astype(BF16))
    d_in[...] = dx_st
    for pair in range(heads // 2):
        at = slice(pair * pair_width, (pair + 1) * pair_width)
        xp, dyp = xb[:, at], dyb[:, at]
        none = jnp.zeros_like(xp)
        x_first, x_second = jnp.where(first, xp, none), jnp.where(first, none, xp)
        g_top = dot_nt(jnp.concatenate([x_first[:half], x_second[:half]], axis=0), dyp)
        g_low = dot_nt(jnp.concatenate([x_first[half:], x_second[half:]], axis=0), dyp[half:])
        tops, lows, d_top, d_low = [], [], 0.0, 0.0
        for which in (0, 1):
            h = 2 * pair + which
            own = slice(which * half, (which + 1) * half)
            col = cols[:, h : h + 1]
            row = cum[h : h + 1, :]
            top = jnp.exp2((row - col[:half]) + mask_bias[:half, :])
            low = jnp.exp2((row[:, half:] - col[half:]) + mask_bias[half:, half:])
            p_top = top * g_top[own]
            p_low = low * g_low[own]
            d_top = d_top + p_top
            d_low = d_low + p_low
            m_top = p_top * scores[:half, :]
            m_low = p_low * scores[half:, half:]
            late = jnp.sum(m_top[:, half:], axis=0, keepdims=True) + jnp.sum(m_low, axis=0, keepdims=True)
            row_sums[h : h + 1, :half] = jnp.sum(m_top[:, :half], axis=0, keepdims=True)
            row_sums[h : h + 1, half:] = late
            parts = split3(jnp.concatenate([m_top[:, :half] + m_top[:, half:], m_low], axis=0))
            col_h = col_h + dot_nt((head_row == h).astype(BF16), jnp.concatenate(parts, axis=1))
            tops.append((top * scores[:half, :]).astype(BF16))
            lows.append((low * scores[half:, half:]).astype(BF16))
        d_scores[:half, :] += d_top
        d_scores[half:, half:] += d_low
        top = dot(jnp.concatenate(tops, axis=0), dyp)
        low = dot(jnp.concatenate(lows, axis=0), dyp[half:])
        d_in[:half, at] += jnp.where(first, top[:half], top[half:])
        d_in[half:, at] += jnp.where(first, low[:half], low[half:])

    everywhere = slice(0, channels)
    dyf = dy_ref[0].astype(F32)
    cx = cx_ref[0]
    sig = sigmoid(cx)
    gx_ref[5:6, :] += jnp.sum(dyf * (cx * sig).astype(BF16).astype(F32), axis=0, keepdims=True)
    d_cx = (d_in[...] + skip_ref[...] * dyf) * (sig * (1.0 + cx * (1.0 - sig)))
    dx_ref[0] = conv_back(d_cx, x_ref[0], ds_x, everywhere, taps_x_ref, gx_ref).astype(BF16)

    dsb = d_scores[...].astype(BF16)
    d_b = d_b + dot(dsb, c_mat)
    d_c = d_c + dot_tn(dsb, b_mat)
    sig = sigmoid(cbc)
    d_cbc = jnp.concatenate([d_b, d_c], axis=1) * (sig * (1.0 + cbc * (1.0 - sig)))
    every = slice(0, 2 * n)
    dbc_ref[0, :, every] = conv_back(d_cbc, bc_ref[0], ds_bc, every, taps_bc_ref, gbc_ref).astype(BF16)

    used_h = col_h + state_h
    diff_h = row_sums[...] - col_h + out_h
    since = (rows >= places).astype(F32)
    before = (rows < places).astype(F32)
    d_rate = (
        jnp.dot(diff_h, since, precision=EXACT, preferred_element_type=F32)
        + jnp.dot(state_h, before, precision=EXACT, preferred_element_type=F32)
        + carried
    )
    sig_dt = sigmoid(biased)
    ratio = jnp.where(step < 1e-30, 1.0, sig_dt / jnp.maximum(step, 1e-30))
    d_raw = used_h * ratio - jnp.exp(a_log) * sig_dt * d_rate
    lanes = dbc_ref.shape[2] - 2 * n
    mine = lax.broadcasted_iota(jnp.int32, (heads, lanes), 0) + lax.axis_index("tensor") * heads
    own = (lax.broadcasted_iota(jnp.int32, (heads, lanes), 1) == mine).astype(BF16)
    dbc_ref[0, :, 2 * n :] = dot_tn(d_raw.astype(BF16), own).astype(BF16)
    gh_ref[:, 0:1] += jnp.sum(d_raw, axis=1, keepdims=True)
    gh_ref[:, 1:2] += jnp.sum(d_rate * rate, axis=1, keepdims=True)


def row_marks(segments):
    seqs, length = segments.shape
    blocks = length // BLOCK
    lags = []
    for lag in (1, 2, 3):
        earlier = jnp.pad(segments, ((0, 0), (lag, 0)), constant_values=-1)[:, :length]
        lags.append(earlier == segments)
    grouped = segments.reshape(seqs, blocks, BLOCK)
    before = jnp.pad(segments, ((0, 0), (1, 0)), constant_values=-1)[:, :length].reshape(seqs, blocks, BLOCK)
    reads = (grouped == before[:, :, :1]).reshape(seqs, length)
    last = (grouped == grouped[:, :, -1:]).reshape(seqs, length)
    rows = [m.astype(F32) for m in (*lags, reads, last, segments)]
    return jnp.stack(rows + [jnp.zeros_like(rows[0])] * 2, axis=1)


def spread_matrix(heads, channels):
    width = channels // heads
    return (np.arange(heads)[:, None] == np.arange(channels)[None, :] // width).astype(np.float32)


def pick_matrix(heads, channels):
    spread = spread_matrix(heads, channels)
    out = np.zeros((128, 2 * channels), np.float32)
    for part in range(4):
        at = slice(part // 2 * channels, (part // 2 + 1) * channels)
        out[part * heads : (part + 1) * heads, at] = spread
    return out


def shared_specs(channels, n2, heads):
    full = lambda *shape: pl.BlockSpec(shape, lambda *i: (0,) * len(shape))
    return [
        full(5, channels),
        full(5, n2),
        full(1, heads),
        full(1, heads),
        full(1, channels),
        full(heads, channels),
        full(128, 2 * channels),
    ]


def forward_scratch(channels, n2):
    return [
        pltpu.VMEM((BLOCK + 8, channels), F32),
        pltpu.VMEM((BLOCK + 8, n2), F32),
        pltpu.VMEM((n2 // 2, channels), F32),
        pltpu.VMEM((BLOCK, BLOCK), F32),
    ]


def forward_kernel(x_ref, bc_ref, dt_ref, *refs):
    y_ref = refs[8]
    forward_block(pl.program_id(1), x_ref[0], bc_ref[0], dt_ref[0], *refs[:8], y_ref.at[0], *refs[9:])


def ssd_forward(x, bc, dt, marks, shared):
    seqs, length, channels = x.shape
    n2, heads = bc.shape[2], dt.shape[1]
    blocks = length // BLOCK
    tok = lambda w: pl.BlockSpec((1, BLOCK, w), lambda s, c: (s, c, 0))
    head = lambda w: pl.BlockSpec((1, w, BLOCK), lambda s, c: (s, 0, c))
    return pl.pallas_call(
        forward_kernel,
        grid=(seqs, blocks),
        in_specs=[tok(channels), tok(n2), head(heads), head(8)] + shared_specs(channels, n2, heads),
        out_specs=[
            tok(channels),
            tok(channels),
            tok(n2),
            pl.BlockSpec((1, 1, n2 // 2, channels), lambda s, c: (s, c, 0, 0)),
        ],
        out_shape=[
            jax.ShapeDtypeStruct((seqs, length, channels), F32),
            jax.ShapeDtypeStruct((seqs, length, channels), F32),
            jax.ShapeDtypeStruct((seqs, length, n2), F32),
            jax.ShapeDtypeStruct((seqs, blocks, n2 // 2, channels), BF16),
        ],
        scratch_shapes=forward_scratch(channels, n2),
        compiler_params=pltpu.CompilerParams(vmem_limit_bytes=48 * 2**20),
        name="ssd_forward",
    )(x, bc, dt, marks, *shared)


def backward_kernel(*refs):
    backward_block(pl.program_id(0), pl.program_id(1), *refs)


def backward_scratch(channels, n2, heads):
    return [
        pltpu.VMEM((3, BLOCK + 8, channels), F32),
        pltpu.VMEM((3, BLOCK + 8, n2), F32),
        pltpu.VMEM((n2 // 2, channels), F32),
        pltpu.VMEM((BLOCK, BLOCK), F32),
        pltpu.VMEM((BLOCK, BLOCK), F32),
        pltpu.VMEM((BLOCK, channels), F32),
        pltpu.VMEM((heads, BLOCK), F32),
    ]


def backward_specs(channels, n2, heads, small, place):
    tok = lambda w: pl.BlockSpec((1, BLOCK, w), lambda *i: (*place(*i), 0))
    full = lambda *shape: pl.BlockSpec(shape, lambda *i: (0,) * len(shape))
    ins = [tok(channels)] * 3 + [tok(n2)] * 2 + [
        pl.BlockSpec((1, heads, BLOCK), lambda *i: (place(*i)[0], 0, place(*i)[1])),
        pl.BlockSpec((1, 8, BLOCK), lambda *i: (place(*i)[0], 0, place(*i)[1])),
        pl.BlockSpec((1, 1, n2 // 2, channels), lambda *i: (*place(*i), 0, 0)),
    ]
    ins += shared_specs(channels, n2, heads)
    return ins, [tok(channels), tok(small), full(8, channels), full(8, n2), full(heads, 128)]


def backward_outs(seqs, length, channels, n2, heads, small):
    return [
        jax.ShapeDtypeStruct((seqs, length, channels), BF16),
        jax.ShapeDtypeStruct((seqs, length, small), BF16),
        jax.ShapeDtypeStruct((8, channels), F32),
        jax.ShapeDtypeStruct((8, n2), F32),
        jax.ShapeDtypeStruct((heads, 128), F32),
    ]


def ssd_backward(small, dy, x, cx, bc, cbc, dt, marks, states, shared):
    seqs, length, channels = x.shape
    n2, heads = bc.shape[2], dt.shape[1]
    blocks = length // BLOCK
    ins, outs = backward_specs(channels, n2, heads, small, lambda s, c: (s, blocks - 1 - c))
    return pl.pallas_call(
        backward_kernel,
        grid=(seqs, blocks),
        in_specs=ins,
        out_specs=outs,
        out_shape=backward_outs(seqs, length, channels, n2, heads, small),
        scratch_shapes=backward_scratch(channels, n2, heads),
        compiler_params=pltpu.CompilerParams(vmem_limit_bytes=56 * 2**20),
        name="ssd_backward",
    )(dy, x, cx, bc, cbc, dt, marks, states, *shared)


def ring_place(n):
    dp = lax.axis_index("dp")
    z, y = dp // 2, dp % 2

    def at(place):
        q = (place + 4 * n) % n
        return 2 * q + (q // (n // 2)) * (2 * n - 1 - 4 * q)

    return z + y * (n - 1 - 2 * z), at


def tensor_place():
    t = lax.axis_index("tensor")
    return t, t + 1 - 2 * (t % 2), (t + 2) % 4


def greet(n, more=()):
    place, at = ring_place(n)
    _, other, across = tensor_place()
    sem = pltpu.get_barrier_semaphore()
    targets = [{"dp": at(place + 1)}, {"dp": at(place - 1)}, {"tensor": other}, {"tensor": across}, *more]
    for target in targets:
        pl.semaphore_signal(sem, inc=1, device_id=target, device_id_type=MESH)
    pl.semaphore_wait(sem, len(targets))


def remote(src, dst, send_sem, recv_sem, target):
    return pltpu.make_async_remote_copy(
        src_ref=src, dst_ref=dst, send_sem=send_sem, recv_sem=recv_sem, device_id=target, device_id_type=MESH
    )


def span(first, count, unit):
    return pl.ds(pl.multiple_of(first, unit), count)


class RingGather:
    def __init__(self, n, parts, keep, sems):
        self.n, self.parts, self.keep = n, parts, keep
        self.send_sem, self.recv_sem = sems
        self.place, self.at = ring_place(n)

    def copy(self, way, part, step):
        sign = 1 - 2 * way
        ref = self.keep(way, part, self.at(self.place - sign * step))
        return remote(
            ref,
            ref,
            self.send_sem.at[way, part, step],
            self.recv_sem.at[way, part, step],
            {"dp": self.at(self.place + sign)},
        )

    def step(self, k):
        for part in range(self.parts):
            for way in (0, 1):
                if k > 0:
                    self.copy(way, part, k - 1).wait_recv()
                if k < self.n - 1:
                    self.copy(way, part, k).start()

    def later(self, k):
        for part in range(self.parts):
            for way in (0, 1):
                self.copy(way, part, k - 1).wait_recv()

                @pl.when(k < self.n - 1)
                def _():
                    self.copy(way, part, k).start()

    def finish(self):
        for k in range(self.n - 1):
            for part in range(self.parts):
                for way in (0, 1):
                    self.copy(way, part, k).wait_send()


class RowGather:
    def __init__(self, keep, sems):
        self.keep = keep
        self.send_sem, self.recv_sem = sems
        self.me, self.other, self.across = tensor_place()

    def copy(self, kind, part):
        ref = self.keep(part, self.across if kind == 2 else self.me)
        target = self.across if kind == 0 else self.other
        return remote(
            ref, ref, self.send_sem.at[kind, part], self.recv_sem.at[kind, part], {"tensor": target}
        )

    def start(self, part):
        self.copy(0, part).start()
        self.copy(1, part).start()

    def forward(self, part):
        self.copy(0, part).wait_recv()
        self.copy(2, part).start()

    def wait(self, part):
        self.copy(1, part).wait_recv()
        self.copy(2, part).wait_recv()

    def finish(self, parts):
        for part in range(parts):
            for kind in range(3):
                self.copy(kind, part).wait_send()


def all_kernel(n, *refs):
    (hidden_ref, g_ref, wzx_ref, wbc_ref, wout_ref, gain_ref, gate_ref, marks_ref), refs = refs[:8], refs[8:]
    shared, refs = refs[:7], refs[7:]
    (u_out, gf_out, wx_out, wz_out, wb_out, wo_out), refs = refs[:6], refs[6:]
    (cx_ref, x_ref, cbc_ref, bc_ref, dt_ref, states_ref), refs = refs[:6], refs[6:]
    (normed_ref, dz_ref, dy_ref, grad_ref, scale_ref), refs = refs[:5], refs[5:]
    scratch, refs = refs[:4], refs[4:]
    (u, wx, wz, wo, wb, wb_own, wdt, g_cols, y, z, dn, sums), refs = refs[:12], refs[12:]
    (load_sem, keep_sem, stream_sem), sems = refs[:3], refs[3:]

    i = pl.program_id(0)
    rows, width = wzx_ref.shape[1:]
    out_rows, out_cols = wout_ref.shape
    seqs, piece, model = hidden_ref.shape
    length = 4 * piece
    blocks = length // BLOCK
    heads = dt_ref.shape[1]
    n2 = bc_ref.shape[2]
    small_cols = wb.shape[1]
    dp = lax.axis_index("dp")
    place, at = ring_place(n)
    me, other, across = tensor_place()
    core = me % 2
    facing = (other + 2) % 4

    def keep_wide(ref):
        def keep(way, part, d):
            return ref.at[span(d * rows, rows, 16), pl.ds(way * width // 2 + part * width // 4, width // 4)]

        return keep

    def keep_out(way, part, d):
        first = way * out_rows // 2 + part * out_rows // 4
        return wo.at[pl.ds(first, out_rows // 4), span(d * out_cols, out_cols, 128)]

    def keep_small(way, part, d):
        return wb.at[span(d * rows + core * rows // 2 + way * rows // 4, rows // 4, 16), :]

    def keep_rows(part, t):
        if part < seqs:
            return u.at[span(part * length + t * piece, piece, 16), :]
        return gf_out.at[part - seqs, span(t * piece, piece, 16), :]

    x_ring = RingGather(n, 2, keep_wide(wx), sems[0:2])
    small = RingGather(n, 1, keep_small, sems[2:4])
    z_ring = RingGather(n, 2, keep_wide(wz), sems[4:6])
    out_ring = RingGather(n, 2, keep_out, sems[6:8])
    token_rows = RowGather(keep_rows, sems[8:10])
    halves_send, halves_recv, sums_send, sums_recv = sems[10:14]

    def half(ahead, whose):
        d = (dp + ahead) % n
        ref = wb.at[span(d * rows + whose * rows // 2, rows // 2, 16), :]
        return remote(ref, ref, halves_send.at[ahead], halves_recv.at[ahead], {"tensor": other})

    def sums_copy(kind):
        ref = sums.at[me]
        target = {"tensor": (other, across, facing)[kind]}
        return remote(ref, ref, sums_send.at[kind], sums_recv.at[kind], target)

    keeps = [
        pltpu.make_async_copy(src, dst, keep_sem.at[j])
        for j, (src, dst) in enumerate(((wx, wx_out), (wb, wb_out), (wz, wz_out), (u, u_out), (wo, wo_out)))
    ]

    def streams(k):
        return [
            pltpu.make_async_copy(
                gf_out.at[:, :, span(at(place - (1 - 2 * way) * k) * out_cols, out_cols, 128)],
                g_cols.at[way],
                stream_sem.at[way],
            )
            for way in (0, 1)
        ]

    def start(copies):
        for copy in copies:
            copy.start()

    def wait(copies):
        for copy in copies:
            copy.wait()

    @pl.when(i == 0)
    def _():
        def held(s, h):
            return z.at[pl.ds((2 * s + h) * piece, piece), :]

        halves = [(s, h) for s in range(seqs) for h in (0, 1)]
        cut = lambda h: pl.ds(h * (model // 2), model // 2)
        own = [
            (wzx_ref.at[1], wx.at[span(dp * rows, rows, 16), :]),
            (wbc_ref, wb_own),
            (wzx_ref.at[0], wz.at[span(dp * rows, rows, 16), :]),
            (wout_ref, wo.at[:, span(dp * out_cols, out_cols, 128)]),
        ]
        own += [(hidden_ref.at[s, :, cut(h)], held(seqs + s, h)) for s, h in halves]
        own += [(g_ref.at[s, :, cut(h)], held(s, h)) for s, h in halves]
        loads = [pltpu.make_async_copy(a, b, load_sem.at[j]) for j, (a, b) in enumerate(own)]
        first = 4 + 2 * seqs
        stores = [
            pltpu.make_async_copy(
                held(s, h), gf_out.at[s, span(me * piece, piece, 16), cut(h)], load_sem.at[first + 2 * seqs + j]
            )
            for j, (s, h) in enumerate(halves)
        ]
        start(loads)
        greet(n, [{"tensor": facing}])
        loads[0].wait()
        x_ring.step(0)
        loads[1].wait()
        columns = wb_own.shape[1]
        tail = columns // 128 * 128
        mine = span(dp * rows, rows, 16)
        wb[mine, :tail] = wb_own[:, :tail]
        wb[mine, tail:] = jnp.zeros((rows, small_cols - tail), BF16)
        wb[mine, tail:columns] = wb_own[:, tail:]
        small.step(0)
        wait(loads[4:first])
        for s in range(seqs):
            left = z[pl.ds((2 * (seqs + s)) * piece, piece), :].astype(F32)
            right = z[pl.ds((2 * (seqs + s) + 1) * piece, piece), :].astype(F32)
            squares = jnp.sum(left * left + right * right, axis=1, keepdims=True)
            scale = lax.rsqrt(squares / model + EPS)
            scale_ref[s] = jnp.broadcast_to(scale, (piece, 128))
            to = span(s * length + me * piece, piece, 16)
            u[to, cut(0)] = (left * scale * gain_ref[:, cut(0)]).astype(BF16)
            u[to, cut(1)] = (right * scale * gain_ref[:, cut(1)]).astype(BF16)
            token_rows.start(s)
        wait(loads[first:])
        start(stores)
        wait(loads[2:4])
        wait(stores)
        for k in range(1, n):
            x_ring.step(k)
            small.step(k)
            if k == n - 1:
                z_ring.step(0)
            if k == n // 2:
                token_rows.forward(0)
                token_rows.start(seqs)
        for ahead in range(1, n):
            half(ahead, core).start()
        for ahead in range(1, n):
            half(ahead, 1 - core).wait_recv()
        token_rows.wait(0)
        start(keeps[:2])
        lanes = small_cols - n2
        pick = lax.broadcasted_iota(jnp.int32, (heads, lanes), 1) == (
            lax.broadcasted_iota(jnp.int32, (heads, lanes), 0) + me * heads
        )
        wdt[...] = dot_nt(pick.astype(BF16), wb[:, n2:]).astype(BF16)

    b = i - 1

    @pl.when((b >= 0) & (b < n))
    def _():
        @pl.when(b < n - 1)
        def _():
            z_ring.later(b + 1)

        @pl.when(b == n - 2)
        def _():
            out_ring.step(0)

        @pl.when(b == n - 1)
        def _():
            keeps[2].start()
            out_ring.step(1)

        @pl.when(b == 0)
        def _():
            token_rows.forward(1)
            token_rows.start(seqs + 1)

        @pl.when(b == blocks)
        def _():
            token_rows.wait(1)
            keeps[3].start()

        at_block = span(b * BLOCK, BLOCK, BLOCK)
        tokens = u[at_block, :]
        x = dot(tokens, wx[...])
        bc = dot(tokens, wb[:, :n2])
        dt = dot_nt(wdt[...], tokens)
        x_ref[0] = x.astype(BF16)
        bc_ref[0] = bc.astype(BF16)
        dt_ref[0] = dt
        forward_block(
            b % blocks, x, bc, dt, marks_ref, *shared, y.at[at_block, :], cx_ref, cbc_ref, states_ref, *scratch
        )

    c = i - (n + 1)

    def add_shard(k):
        wait(streams(k))
        for way in (0, 1):
            e = pl.ds(way * (out_rows // 2), out_rows // 2)
            d = at(place - (1 - 2 * way) * k)
            cols = g_cols[way].reshape(seqs * length, out_cols)
            value = dot_nt(cols, wo[e, span(d * out_cols, out_cols, 128)])

            @pl.when(k == 0)
            def _():
                dn[:, e] = value

            @pl.when(k > 0)
            def _():
                dn[:, e] += value

    @pl.when((c >= 0) & (c < n - 2))
    def _():
        @pl.when(c == 0)
        def _():
            token_rows.forward(seqs)
            token_rows.forward(seqs + 1)
            token_rows.wait(seqs)
            token_rows.wait(seqs + 1)
            start(streams(0))
            add_shard(0)
            start(streams(1))

        @pl.when((c >= 1) & (c <= 4))
        def _():
            part = span((c - 1) * (seqs * length // 4), seqs * length // 4, 16)
            z[part, :] = dot(u[part, :], wz[...]).astype(BF16)

        add_shard(c + 1)
        start(streams(c + 2))
        out_ring.later(c + 2)

        @pl.when(c == n - 3)
        def _():
            add_shard(n - 1)
            keeps[4].start()

            def block_sums(e, _):
                part = span(e * BLOCK, BLOCK, BLOCK)
                zf = z[part, :].astype(F32)
                gated = y[part, :] * (zf * sigmoid(zf))
                squares = jnp.sum(gated * gated, axis=1, keepdims=True)
                inner = jnp.sum(gate_ref[...] * dn[part, :] * gated, axis=1, keepdims=True)
                lane = lax.broadcasted_iota(jnp.int32, (1, 128), 1)
                both = jnp.where(lane == 0, squares, jnp.where(lane == 1, inner, 0.0))
                sums[me, :, part] = both.T[0:8, :]
                return 0

            lax.fori_loop(0, n, block_sums, 0)
            for kind in range(3):
                sums_copy(kind).start()

    e = i - (2 * n - 1)

    @pl.when(e >= 0)
    def _():
        @pl.when(e == 0)
        def _():
            for kind in range(3):
                sums_copy(kind).wait_recv()
            grad_ref[...] = jnp.zeros_like(grad_ref)

        part = span(e * BLOCK, BLOCK, BLOCK)
        whole = (sums[0, :, part] + sums[1, :, part]) + (sums[2, :, part] + sums[3, :, part])
        cols = jnp.concatenate([whole, jnp.zeros((120, BLOCK), F32)], axis=0).T / (4 * width)
        inverse = lax.rsqrt(cols[:, 0:1] + EPS)
        zf = z[part, :].astype(F32)
        sig = sigmoid(zf)
        silu = zf * sig
        yf = y[part, :]
        dnf = dn[part, :]
        gain = gate_ref[...]
        gated = yf * silu
        scaled_gated = gated * inverse
        normed_ref[...] = (scaled_gated * gain).astype(BF16)
        grad_ref[...] += jnp.sum(dnf * scaled_gated, axis=0, keepdims=True)
        d_gated = inverse * (dnf * gain) - gated * (inverse * inverse * inverse * cols[:, 1:2])
        dy_ref[...] = (d_gated * silu).astype(BF16)
        dz_ref[...] = (d_gated * yf * (sig * (1.0 + zf * (1.0 - sig)))).astype(BF16)

        @pl.when(e == n - 1)
        def _():
            wait(keeps)
            for ring in (x_ring, small, z_ring, out_ring):
                ring.finish()
            token_rows.finish(2 * seqs)
            for ahead in range(1, n):
                half(ahead, core).wait_send()
            for kind in range(3):
                sums_copy(kind).wait_send()


def forward_all(n, hidden, g, w_zx, w_bc, w_out, pre_gain, gate_gain, marks, shared):
    seqs, piece, model = hidden.shape
    rows, width = w_zx.shape[1:]
    out_rows, out_cols = w_out.shape
    length = 4 * piece
    tokens = seqs * length
    blocks = length // BLOCK
    n2 = shared[1].shape[1]
    heads = shared[2].shape[1]
    columns = w_bc.shape[1]
    small = columns + -columns % 128
    sem = pltpu.SemaphoreType.DMA
    ring = [sem((2, 2, n - 1))] * 2
    anywhere = pl.BlockSpec(memory_space=pl.ANY)
    whole = lambda *shape: pl.BlockSpec(shape, lambda i: (0,) * len(shape))
    b = lambda i: jnp.minimum(jnp.maximum(i - 1, 0), n - 1)
    e = lambda i: jnp.maximum(i - (2 * n - 1), 0)
    tok = lambda w: pl.BlockSpec((1, BLOCK, w), lambda i: (b(i) // blocks, b(i) % blocks, 0))
    gate = pl.BlockSpec((BLOCK, width), lambda i: (e(i), 0))
    out_shape = [
        ((tokens, model), BF16),
        ((seqs, length, model), BF16),
        ((rows * n, width), BF16),
        ((rows * n, width), BF16),
        ((rows * n, small), BF16),
        ((out_rows, out_cols * n), BF16),
        ((seqs, length, width), F32),
        ((seqs, length, width), BF16),
        ((seqs, length, n2), F32),
        ((seqs, length, n2), BF16),
        ((seqs, heads, length), F32),
        ((seqs, blocks, n2 // 2, width), BF16),
        ((tokens, width), BF16),
        ((tokens, width), BF16),
        ((tokens, width), BF16),
        ((1, width), F32),
        ((seqs, piece, 128), F32),
    ]
    return pl.pallas_call(
        functools.partial(all_kernel, n),
        grid=(3 * n - 1,),
        in_specs=[anywhere] * 5
        + [
            whole(1, model),
            whole(1, width),
            pl.BlockSpec((1, 8, BLOCK), lambda i: (b(i) // blocks, 0, b(i) % blocks)),
        ]
        + shared_specs(width, n2, heads),
        out_specs=[anywhere] * 6
        + [tok(width), tok(width), tok(n2), tok(n2)]
        + [pl.BlockSpec((1, heads, BLOCK), lambda i: (b(i) // blocks, 0, b(i) % blocks))]
        + [pl.BlockSpec((1, 1, n2 // 2, width), lambda i: (b(i) // blocks, b(i) % blocks, 0, 0))]
        + [gate] * 3
        + [whole(1, width), whole(seqs, piece, 128)],
        out_shape=[jax.ShapeDtypeStruct(*s) for s in out_shape],
        scratch_shapes=forward_scratch(width, n2)
        + [
            pltpu.VMEM((tokens, model), BF16),
            pltpu.VMEM((rows * n, width), BF16),
            pltpu.VMEM((rows * n, width), BF16),
            pltpu.VMEM((out_rows, out_cols * n), BF16),
            pltpu.VMEM((rows * n, small), BF16),
            pltpu.VMEM(w_bc.shape, BF16),
            pltpu.VMEM((heads, rows * n), BF16),
            pltpu.VMEM((2, seqs, length, out_cols), BF16),
            pltpu.VMEM((tokens, width), F32),
            pltpu.VMEM((tokens, width), BF16),
            pltpu.VMEM((tokens, width), F32),
            pltpu.VMEM((4, 8, tokens), F32),
            sem((4 + 6 * seqs,)),
            sem((5,)),
            sem((2,)),
        ]
        + ring + [sem((2, 1, n - 1))] * 2 + ring + ring
        + [sem((3, 2 * seqs))] * 2 + [sem((n,))] * 2 + [sem((3,))] * 2,
        compiler_params=pltpu.CompilerParams(
            collective_id=0, has_side_effects=True, vmem_limit_bytes=63 * 2**20
        ),
        name="forward_all",
    )(hidden, g, w_zx, w_bc, w_out, pre_gain, gate_gain, marks, *shared)


class RingScatter:
    def __init__(self, n, terms, slots, sems, ways=2, sign=1):
        self.n, self.terms, self.slots, self.ways, self.sign = n, terms, slots, ways, sign
        self.send_sem, self.recv_sem = sems
        self.place, self.at = ring_place(n)

    def turn(self, way):
        return self.sign * (1 - 2 * way)

    def owner(self, way, k):
        return self.at(self.place - self.turn(way) * (1 + k))

    def copy(self, way, k):
        return remote(
            self.slots.at[way, k],
            self.slots.at[way, k + 1],
            self.send_sem.at[way, k],
            self.recv_sem.at[way, k],
            {"dp": self.at(self.place + self.turn(way))},
        )

    def step(self, way, k):
        @pl.when(k == 0)
        def _():
            self.slots[way, 0] = self.terms[way].astype(BF16)

        @pl.when(k > 0)
        def _():
            self.copy(way, k - 1).wait_recv()

            @pl.when(k < self.n - 1)
            def _():
                self.slots[way, k] = (self.terms[way].astype(F32) + self.slots[way, k].astype(F32)).astype(BF16)

        @pl.when(k < self.n - 1)
        def _():
            self.copy(way, k).start()

    def last(self, way):
        return self.terms[way].astype(F32) + self.slots[way, self.n - 1].astype(F32)

    def finish(self):
        for k in range(self.n - 1):
            for way in range(self.ways):
                self.copy(way, k).wait_send()


class RowScatter:
    def __init__(self, parts, value, hold, sems):
        self.parts, self.value, self.hold = parts, value, hold
        self.send_sem, self.recv_sem = sems
        self.me, self.other, self.across = tensor_place()

    def copy(self, kind, part):
        src, dst = ((0, 1), (1, 2), (0, 3))[kind]
        return remote(
            self.hold.at[src, part],
            self.hold.at[dst, part],
            self.send_sem.at[kind, part],
            self.recv_sem.at[kind, part],
            {"tensor": self.across if kind == 1 else self.other},
        )

    def stage(self, j):
        late = j // (2 * self.parts)
        near = j - 2 * self.parts
        stage = (1 - late) * (j % 2) + late * (2 + near // self.parts)
        return stage, (1 - late) * (j // 2) + late * (near % self.parts)

    def owner(self, j):
        stage, part = self.stage(j)
        x, core = self.me // 2, self.me % 2
        return 2 * ((x + 1 - stage // 2) % 2) + (core + 1 - stage % 2) % 2, part

    def step(self, j, store, wait=True):
        stage, part = self.stage(j)

        @pl.when(stage == 0)
        def _():
            self.hold[0, part] = self.value[...].astype(BF16)
            self.copy(0, part).start()

        @pl.when(stage == 1)
        def _():
            self.copy(0, part).wait_recv()
            self.hold[1, part] = (self.value[...].astype(F32) + self.hold[1, part].astype(F32)).astype(BF16)
            self.copy(1, part).start()

        @pl.when(stage == 2)
        def _():
            self.copy(0, part).wait_send()
            self.hold[0, part] = self.value[...].astype(BF16)
            self.copy(2, part).start()

        @pl.when(stage == 3)
        def _():
            value = self.value[...].astype(F32)
            store(part, value + self.arrived(part) if wait else value)

    def arrived(self, part):
        self.copy(2, part).wait_recv()
        self.copy(1, part).wait_recv()
        return self.hold[3, part].astype(F32) + self.hold[2, part].astype(F32)

    def finish(self):
        for part in range(self.parts):
            for kind in (1, 2):
                self.copy(kind, part).wait_send()


def back_kernel(n, *refs):
    (normed_ref, g_ref, u_ref, dz_ref, wo_ref), refs = refs[:5], refs[5:]
    ins, refs = refs[:15], refs[15:]
    (out_ref, gout_ref, gz_ref), refs = refs[:3], refs[3:]
    outs, refs = refs[:5], refs[5:]
    scratch, refs = refs[:7], refs[7:]
    normed, dz, wo, g_cols, u_cols, out_slots, z_slots, hold, terms, mixed, load_sem, stream_sem, out_sem = refs[:13]
    sems = refs[13:]

    k = pl.program_id(0)
    blocks = 4
    piece = out_ref.shape[1]
    length = blocks * BLOCK
    count = g_ref.shape[1] // n
    half = gz_ref.shape[1] // 2
    place, at = ring_place(n)

    loads = [
        pltpu.make_async_copy(src, dst, load_sem.at[i])
        for i, (src, dst) in enumerate(((normed_ref, normed), (dz_ref, dz), (wo_ref, wo)))
    ]

    def streams(k):
        copies = []
        for way in (0, 1):
            d = at(place - (1 - 2 * way) * (1 + k))
            for i, (src, dst) in enumerate(((g_ref, g_cols), (u_ref, u_cols))):
                copies.append(
                    pltpu.make_async_copy(
                        src.at[:, span(d * count, count, 128)], dst.at[way], stream_sem.at[i, way]
                    )
                )
        return copies

    @pl.when(k == 0)
    def _():
        for copy in streams(0) + loads:
            copy.start()
        greet(n)

    backward_block(k // blocks, k % blocks, *ins, *outs, *scratch)

    @pl.when(k == 0)
    def _():
        for copy in loads:
            copy.wait()

    for copy in streams(k):
        copy.wait()

    rows = RowScatter(2, mixed, hold, sems[4:6])
    owner = rows.owner(k)
    own_rows = span(owner[1] * length + owner[0] * piece, piece, 16)

    for ring, (from_cols, to_cols) in enumerate(((g_cols, normed), (u_cols, dz))):
        for way in (0, 1):
            value = dot_tn(from_cols[way], to_cols[:, pl.ds(way * half, half)])
            terms[ring, way] = value.astype(BF16)
    mixed[...] = dot(normed[own_rows, :], wo[...]).astype(BF16)

    out_ring = RingScatter(n, terms.at[0], out_slots, sems[0:2])
    z_ring = RingScatter(n, terms.at[1], z_slots, sems[2:4])
    for way in (0, 1):
        out_ring.step(way, k)
        z_ring.step(way, k)

    @pl.when(k < n - 1)
    def _():
        for copy in streams(k + 1):
            copy.start()

    def out_copy(part):
        return pltpu.make_async_copy(hold.at[2, part], out_ref.at[part], out_sem.at[part])

    def store(part, value):
        hold[2, part] = value.astype(BF16)
        out_copy(part).start()

    rows.step(k, store)

    @pl.when(k == n - 1)
    def _():
        for way in (0, 1):
            at = pl.ds(way * half, half)
            gout_ref[at, :] = out_ring.last(way).T
            gz_ref[:, at] = z_ring.last(way)

    @pl.when(k == n - 1)
    def _():
        rows.finish()
        out_ring.finish()
        z_ring.finish()
        for part in range(2):
            out_copy(part).wait()


def backward_all(n, small, piece, normed, g, u, dz, w_out, dy, x, cx, bc, cbc, dt, marks, states, shared):
    seqs, length, channels = x.shape
    n2, heads = bc.shape[2], dt.shape[1]
    tokens, model = g.shape
    count = model // n
    blocks = length // BLOCK
    sem = pltpu.SemaphoreType.DMA
    anywhere = pl.BlockSpec(memory_space=pl.ANY)
    ins, outs = backward_specs(channels, n2, heads, small, lambda k: (k // blocks, blocks - 1 - k % blocks))
    whole = lambda *shape: pl.BlockSpec(shape, lambda k: (0,) * len(shape))
    return pl.pallas_call(
        functools.partial(back_kernel, n),
        grid=(n,),
        in_specs=[anywhere] * 5 + ins,
        out_specs=[anywhere, whole(channels, count), whole(count, channels)] + outs,
        out_shape=[
            jax.ShapeDtypeStruct((seqs, piece, model), BF16),
            jax.ShapeDtypeStruct((channels, count), F32),
            jax.ShapeDtypeStruct((count, channels), F32),
        ]
        + backward_outs(seqs, length, channels, n2, heads, small),
        scratch_shapes=backward_scratch(channels, n2, heads)
        + [
            pltpu.VMEM((tokens, channels), BF16),
            pltpu.VMEM((tokens, channels), BF16),
            pltpu.VMEM((channels, model), BF16),
            pltpu.VMEM((2, tokens, count), BF16),
            pltpu.VMEM((2, tokens, count), BF16),
            pltpu.VMEM((2, n, count, channels // 2), BF16),
            pltpu.VMEM((2, n, count, channels // 2), BF16),
            pltpu.VMEM((4, seqs, piece, model), BF16),
            pltpu.VMEM((2, 2, count, channels // 2), BF16),
            pltpu.VMEM((piece, model), BF16),
            sem((3,)),
            sem((2, 2)),
            sem((seqs,)),
        ]
        + [sem((2, n - 1))] * 4
        + [sem((3, seqs))] * 2,
        compiler_params=pltpu.CompilerParams(
            collective_id=1, has_side_effects=True, vmem_limit_bytes=127 * 2**19
        ),
        name="backward_all",
    )(normed, g, u, dz, w_out, dy, x, cx, bc, cbc, dt, marks, states, *shared)


class Fold:
    def __init__(self, n, total, came, sems):
        self.total, self.came = total, came
        self.send_sem, self.recv_sem = sems
        dp = lax.axis_index("dp")
        _, other, across = tensor_place()
        partners, ahead = [], 1
        while ahead < n:
            partners.append({"dp": dp + ahead * (1 - 2 * ((dp // ahead) % 2))})
            ahead *= 2
        self.over_dp = partners
        self.partners = partners + [{"tensor": other}, {"tensor": across}]

    def copy(self, r):
        return remote(
            self.total.at[r], self.came.at[r], self.send_sem.at[r], self.recv_sem.at[r], self.partners[r]
        )

    def start(self, r):
        self.copy(r).start()

    def take(self, r):
        self.copy(r).wait_recv()
        self.total[r + 1] = self.total[r] + self.came[r]

    def finish(self):
        for r in range(len(self.partners)):
            self.copy(r).wait_send()


def in_kernel(
    n, u_hbm, dz_hbm, dx_hbm, wz_hbm, wx_hbm, wb_hbm, dbc_hbm, gz_hbm, gx_in, gbc_in, gh_in, gate_in, gain_ref,
    din_ref, gx_ref, gb_ref, sums_ref, dots_ref, pre_ref,
    u_ref, dz_ref, dx_ref, wz_ref, wx_ref, wb_ref, dbc_ref,
    x_slots, b_slots, hold, bc_hold, x_terms, b_terms, in_value, bc_value, low, swap, own_in, pre, pre_dp, pre_tensor, total, came, load_sem, u_sem, *sems,
):
    seqs, piece = din_ref.shape[:2]
    tokens, model = u_ref.shape
    length = tokens // seqs
    count = model // n
    half = gx_ref.shape[2] // 2
    me, other, across = tensor_place()
    core = me % 2

    moves = (
        (dbc_hbm, dbc_ref),
        (dx_hbm, dx_ref),
        (dz_hbm, dz_ref),
        (wz_hbm, wz_ref),
        (wx_hbm, wx_ref),
        (wb_hbm, wb_ref),
        (gz_hbm, gx_ref.at[0]),
    )
    loads = [pltpu.make_async_copy(src, dst, load_sem.at[i]) for i, (src, dst) in enumerate(moves)]
    place, at_place = ring_place(n)
    u_copies = []
    for ahead in (-1, 1, -2, 2, -3, 3, 4, 0):
        cols = span(at_place(place + ahead) * count, count, 128)
        u_copies.append(pltpu.make_async_copy(u_hbm.at[:, cols], u_ref.at[:, cols], u_sem.at[ahead + 3]))
    for load in loads[:2] + u_copies[:2] + loads[2:] + u_copies[2:]:
        load.start()

    bc_rows = RowScatter(seqs, bc_value, bc_hold, sems[0:2])
    in_rows = RowScatter(seqs, in_value, hold, sems[2:4])
    x_ring = RingScatter(n, x_terms, x_slots, sems[4:6])
    b_ring = RingScatter(n, b_terms, b_slots, sems[6:8], 1, 1 - 2 * core)
    pair_send, pair_recv, swap_send, swap_recv = sems[8:12]
    dp_send, dp_recv, tensor_send, tensor_recv = sems[14:18]
    fold = Fold(n, total, came, sems[12:14])
    rounds = len(fold.partners)
    pair = remote(low.at[0], low.at[1], pair_send, pair_recv, {"tensor": other})

    total[0] = jnp.zeros_like(total[0])
    total[0, 0:6, :] = gx_in[0:6, :]
    total[0, 6:7, :] = gate_in[...]
    steps = gh_in[...].T
    total[0, 7:8, 0 : steps.shape[1]] = steps[0:1, :]
    total[0, 7:8, 128 : 128 + steps.shape[1]] = steps[1:2, :]
    total[0, 8:13, 0 : gbc_in.shape[1]] = gbc_in[0:5, :]
    pre[...] = jnp.zeros_like(pre)
    dp_now = lax.axis_index("dp")
    greet(
        n,
        fold.over_dp
        + [{"dp": (dp_now + o) % n} for o in range(1, n)]
        + [{"tensor": (me + o) % 4} for o in range(1, 4)],
    )
    def rows_at(t, part):
        return span(part * length + t * piece, piece, 16)

    def bc_store(part, value):
        low[0, part] = value.astype(BF16)

    def bc_step(j):
        t, part = bc_rows.owner(j)
        bc_value[...] = dbc_ref[rows_at(t, part), :].astype(F32)
        bc_rows.step(j, bc_store)

    def add_pre(at):
        pre[...] += jnp.sum(in_value[...] * u_ref[at, :].astype(F32), axis=0, keepdims=True)

    def store(part, value):
        in_value[...] = value + dot_nt(low[0, part], wb_ref[...])
        own_in[part] = in_value[...]
        add_pre(rows_at(me, part))

    def row_term(j):
        at = rows_at(*in_rows.owner(j))
        in_value[...] = dot_nt(dz_ref[at, :], wz_ref[...]) + dot_nt(dx_ref[at, :], wx_ref[...])

    def row_step(j):
        in_rows.step(j, store, wait=False)

        @pl.when(j < 3 * seqs)
        def _():
            add_pre(rows_at(*in_rows.owner(j)))

    def x_term(k):
        for way in (0, 1):
            cols = span(x_ring.owner(way, k) * count, count, 128)
            x_terms[way] = dot_tn(u_ref[:, cols], dx_ref[:, pl.ds(way * half, half)])

    def x_step(k):
        for way in (0, 1):
            x_ring.step(way, k)

    def b_step(k):
        cols = span(b_ring.owner(0, k) * count + core * count // 2, count // 2, 128)
        value = 0.0
        for t, which in ((me, 0), (other, 1)):
            for part in range(seqs):
                value = value + dot_tn(u_ref[rows_at(t, part), cols], low[which, part])
        b_terms[0] = value
        b_ring.step(0, k)

    loads[0].wait()
    for part in range(seqs):
        bc_step(2 * part)
        bc_step(2 * seqs + part)
    loads[1].wait()
    for copy in u_copies[:2]:
        copy.wait()
    x_term(0)
    x_step(0)
    for load in loads[2:] + u_copies[2:]:
        load.wait()
    row_term(0)
    row_step(0)
    for part in range(seqs):
        bc_step(2 * part + 1)

    wide = model // 8
    gain = gain_ref[...]

    def dp_copy(o):
        ref = pre_dp.at[dp_now]
        return remote(ref, ref, dp_send.at[o], dp_recv.at[o], {"dp": (dp_now + o) % n})

    def tensor_copy(o):
        ref = pre_tensor.at[me]
        return remote(ref, ref, tensor_send.at[o], tensor_recv.at[o], {"tensor": (me + o) % 4})

    cross = remote(swap.at[0], swap.at[1], swap_send.at[0], swap_recv.at[0], {"tensor": across})
    back = remote(swap.at[2], swap.at[3], swap_send.at[1], swap_recv.at[1], {"tensor": other})

    def at_step(k, when, what):
        pl.when(k == when)(what)

    def own_bc():
        for part in range(seqs):
            bc_step(3 * seqs + part)
        pair.start()

    def send_pre():
        for i in range(8):
            at = slice(i * wide, (i + 1) * wide)
            pre_dp[dp_now, i : i + 1, :] = pre[:, at] / gain[:, at]
        for o in range(1, n):
            dp_copy(o).start()

    def pass_pre():
        for o in range(1, n):
            dp_copy(o).wait_recv()
        pre_tensor[me] = sum(pre_dp[d] for d in range(n))
        for o in range(1, 4):
            tensor_copy(o).start()

    def take_pre():
        for o in range(1, 4):
            tensor_copy(o).wait_recv()
        pre_ref[...] = (pre_tensor[0] + pre_tensor[1]) + (pre_tensor[2] + pre_tensor[3])

    def send_bc():
        swap[0] = b_ring.last(0)
        cross.start()

    def pass_bc():
        cross.wait_recv()
        swap[2] = swap[0] + swap[1]
        back.start()
        gb_ref[span(core * count // 2, count // 2, 16), :] = swap[2]

    def step(k, _):
        at_step(k, 5, send_pre)
        at_step(k, n - 1, send_bc)

        @pl.when(2 * k - 1 < 4 * seqs)
        def _():
            row_term(2 * k - 1)
            row_step(2 * k - 1)

        x_term(k)
        x_step(k)
        at_step(k, 2, pair.wait_recv)

        @pl.when((k >= 2) & (k <= 6))
        def _():
            b_step(jnp.maximum(k - 2, 2 * (k - 3)))

        @pl.when(2 * k < 4 * seqs)
        def _():
            row_term(2 * k)
            row_step(2 * k)

        at_step(k, 1, own_bc)

        @pl.when((k >= 4) & (k <= 6))
        def _():
            b_step(2 * (k - 3) + 1)

        at_step(k, 6, pass_pre)
        at_step(k, n - 1, pass_bc)
        at_step(k, n - 1, take_pre)
        for r in range(rounds + 1):

            @pl.when(k == r + 1)
            def _():
                if r > 0:
                    fold.take(r - 1)
                if r < rounds:
                    fold.start(r)

        return 0

    lax.fori_loop(1, n, step, 0)
    for way in (0, 1):
        gx_ref[1, :, pl.ds(way * half, half)] = x_ring.last(way)
    sums_ref[0:8, :] = total[rounds - 2, 0:8, :]
    sums_ref[8:16, :] = total[rounds, 8:16, :]
    for part in range(seqs):
        value = own_in[part] + in_rows.arrived(part)
        din_ref[part] = value.astype(BF16)
        inner = jnp.sum(value * u_ref[rows_at(me, part), :].astype(F32), axis=1, keepdims=True)
        dots_ref[part] = jnp.broadcast_to(inner, (piece, 128))
    back.wait_recv()
    gb_ref[span((1 - core) * count // 2, count // 2, 16), :] = swap[3]
    for o in range(1, n):
        dp_copy(o).wait_send()
    for o in range(1, 4):
        tensor_copy(o).wait_send()
    for copy in (pair, cross, back):
        copy.wait_send()
    for part in (bc_rows, in_rows, x_ring, b_ring, fold):
        part.finish()


def scatter_in(n, piece, u, dz, dx, w_z, w_x, w_bc, dbc, grad_z, gx, gbc, gh, grad_gate, gain):
    tokens, model = u.shape
    width = dz.shape[1]
    small = dbc.shape[1]
    seqs = tokens // (4 * piece)
    count = model // n
    rounds = 5
    sem = pltpu.SemaphoreType.DMA
    vmem = pl.BlockSpec(memory_space=pltpu.VMEM)
    anywhere = pl.BlockSpec(memory_space=pl.ANY)
    big = (u, dz, dx, w_z, w_x, w_bc, dbc)
    return pl.pallas_call(
        functools.partial(in_kernel, n),
        in_specs=[anywhere] * 8 + [vmem] * 5,
        out_specs=[vmem] * 6,
        out_shape=[
            jax.ShapeDtypeStruct((seqs, piece, model), BF16),
            jax.ShapeDtypeStruct((2, count, width), F32),
            jax.ShapeDtypeStruct((count, small), F32),
            jax.ShapeDtypeStruct((16, width), F32),
            jax.ShapeDtypeStruct((seqs, piece, 128), F32),
            jax.ShapeDtypeStruct((8, model // 8), F32),
        ],
        scratch_shapes=[pltpu.VMEM(a.shape, BF16) for a in big]
        + [
            pltpu.VMEM((2, n, count, width // 2), BF16),
            pltpu.VMEM((1, n, count // 2, small), BF16),
            pltpu.VMEM((4, seqs, piece, model), BF16),
            pltpu.VMEM((4, seqs, piece, small), BF16),
            pltpu.VMEM((2, count, width // 2), F32),
            pltpu.VMEM((1, count // 2, small), F32),
            pltpu.VMEM((piece, model), F32),
            pltpu.VMEM((piece, small), F32),
            pltpu.VMEM((2, seqs, piece, small), BF16),
            pltpu.VMEM((4, count // 2, small), F32),
            pltpu.VMEM((seqs, piece, model), F32),
            pltpu.VMEM((1, model), F32),
            pltpu.VMEM((n, 8, model // 8), F32),
            pltpu.VMEM((4, 8, model // 8), F32),
            pltpu.VMEM((rounds + 1, 16, width), F32),
            pltpu.VMEM((rounds, 16, width), F32),
            sem((len(big),)),
            sem((n,)),
        ]
        + [sem((3, seqs))] * 4 + [sem((2, n - 1))] * 2 + [sem((1, n - 1))] * 2 + [sem(())] * 2 + [sem((2,))] * 2
        + [sem((rounds,))] * 2 + [sem((n,))] * 2 + [sem((4,))] * 2,
        compiler_params=pltpu.CompilerParams(
            collective_id=2, has_side_effects=True, vmem_limit_bytes=63 * 2**20
        ),
        name="scatter_in",
    )(*big, grad_z, gx, gbc, gh, grad_gate, gain)


def finish_kernel(
    d_in_ref, hidden_ref, cot_ref, mixed_ref, scale_ref, dots_ref, gain_ref, gzx_in, gout_in, gb_in, sums_ref,
    out_ref, d_hidden_ref, gzx_ref, gout_ref, gb_ref, taps_ref, taps_bc_ref,
):
    model = gain_ref.shape[1]
    x = hidden_ref[0].astype(F32)
    scale = scale_ref[0][:, 0:1]
    factor = scale * scale * dots_ref[0][:, 0:1] / model
    d_hidden_ref[0] = cot_ref[0].astype(F32) + scale * (gain_ref[...] * d_in_ref[0].astype(F32)) - x * factor
    out_ref[0] = (x + mixed_ref[0].astype(F32)).astype(BF16)
    gzx_ref[...] = gzx_in[...]
    gout_ref[...] = gout_in[...]
    gb_ref[...] = gb_in[:, : gb_ref.shape[1]]
    taps_ref[...] = sums_ref[0 : taps_ref.shape[0], :]
    taps_bc_ref[...] = sums_ref[8 : 8 + taps_bc_ref.shape[0], : taps_bc_ref.shape[1]]


def finish(d_in, hidden, cotangent, mixed, scale, dots, gain, grad_zx, grad_out, grad_bc, sums, columns, n2):
    seqs, piece, model = hidden.shape
    count, width = grad_zx.shape[1:]
    steps = 4
    rows = piece // steps
    grid = seqs * steps
    piece_rows = lambda w: pl.BlockSpec((1, rows, w), lambda i: (i // steps, i % steps, 0))
    whole = lambda *shape: pl.BlockSpec(shape, lambda i: (0,) * len(shape))
    zx = pl.BlockSpec((1, 2 * count // grid, width), lambda i: (i // (grid // 2), i % (grid // 2), 0))
    down = lambda a, w: pl.BlockSpec((a.shape[0] // grid, w), lambda i: (i, 0))
    return pl.pallas_call(
        finish_kernel,
        grid=(grid,),
        in_specs=[piece_rows(model)] * 4
        + [piece_rows(128)] * 2
        + [whole(1, model), zx, down(grad_out, grad_out.shape[1]), down(grad_bc, grad_bc.shape[1])]
        + [whole(*sums.shape)],
        out_specs=[piece_rows(model)] * 2
        + [zx, down(grad_out, grad_out.shape[1]), down(grad_bc, columns), whole(5, width), whole(5, n2)],
        out_shape=[
            jax.ShapeDtypeStruct(hidden.shape, BF16),
            jax.ShapeDtypeStruct(hidden.shape, F32),
            jax.ShapeDtypeStruct(grad_zx.shape, F32),
            jax.ShapeDtypeStruct(grad_out.shape, F32),
            jax.ShapeDtypeStruct((grad_bc.shape[0], columns), F32),
            jax.ShapeDtypeStruct((5, width), F32),
            jax.ShapeDtypeStruct((5, n2), F32),
        ],
        compiler_params=pltpu.CompilerParams(vmem_limit_bytes=62 * 2**20),
        name="finish",
    )(d_in, hidden, cotangent, mixed, scale, dots, gain, grad_zx, grad_out, grad_bc, sums)


def rms_scale(values):
    return lax.rsqrt(jnp.mean(values * values, axis=-1, keepdims=True) + EPS)


def gather_plain(u, g, w_zx, w_bc, w_out):
    w_zx = lax.all_gather(w_zx, "dp", axis=1, tiled=True)
    return (
        lax.all_gather(u, "tensor", axis=1, tiled=True),
        lax.all_gather(g, "tensor", axis=1, tiled=True),
        w_zx[1],
        w_zx[0],
        lax.all_gather(w_bc, "dp", axis=0, tiled=True),
        lax.all_gather(w_out, "dp", axis=1, tiled=True),
    )


def rows_of(values, piece):
    by_seq = values.reshape(-1, 4 * piece, values.shape[-1])
    return lax.psum_scatter(by_seq, "tensor", scatter_dimension=1, tiled=True)


def scatter_out_plain(piece, normed, g, u, dz, w_out):
    return (
        rows_of(dot(normed, w_out), piece),
        lax.psum_scatter(dot_tn(normed, g), "dp", scatter_dimension=1, tiled=True),
        lax.psum_scatter(dot_tn(u, dz), "dp", scatter_dimension=0, tiled=True),
    )


def scatter_in_plain(piece, u, dz, dx, w_z, w_x, w_bc, dbc):
    low = lax.psum(dbc.astype(F32), "tensor").astype(BF16)
    d_in = rows_of(dot_nt(dz, w_z) + dot_nt(dx, w_x), piece)
    first = lax.axis_index("tensor") * piece
    own = lax.dynamic_slice_in_dim(low.reshape(-1, 4 * piece, low.shape[1]), first, piece, 1)
    d_in = d_in + jnp.einsum("slc,dc->sld", own, w_bc, preferred_element_type=F32)
    return (
        d_in,
        lax.psum_scatter(dot_tn(u, dx), "dp", scatter_dimension=0, tiled=True),
        lax.psum_scatter(dot_tn(u, low), "dp", scatter_dimension=0, tiled=True),
    )


def local(
    n_dp,
    n_tensor,
    hidden,
    pre_gain,
    w_zx,
    w_bcdt,
    conv_x,
    conv_bc,
    dt_bias,
    a_log,
    d_skip,
    gate_gain,
    w_out,
    cotangent,
    segments,
):
    seqs, piece, model = hidden.shape
    length = segments.shape[1]
    tokens = seqs * length
    heads = dt_bias.shape[0]
    channels = conv_x.shape[1]
    n2 = conv_bc.shape[1]
    columns = w_bcdt.shape[1]
    tensor = lax.axis_index("tensor")
    kernels = n_dp == 8 and n_tensor == 4 and seqs == 2 and length == 4 * BLOCK

    x_piece = hidden.astype(F32)
    marks = row_marks(segments)
    spread = jnp.asarray(spread_matrix(heads, channels), BF16)
    skip = jnp.repeat(d_skip, channels // heads)[None]
    pick = jnp.asarray(pick_matrix(heads, channels), BF16)
    shared = (conv_x, conv_bc, dt_bias[None], a_log[None], skip, spread, pick)
    if kernels:
        u, g, w_x, w_z, w_bc, w_o, cx, x, cbc, bc, dt, states, normed, dz, dy, grad_gate, scale_in = forward_all(
            n_dp, hidden, cotangent, w_zx, w_bcdt, w_out, pre_gain[None], gate_gain[None], marks, shared
        )
        g = g.reshape(tokens, model)
    else:
        scale_in = rms_scale(x_piece)
        u_piece = (x_piece * scale_in * pre_gain).astype(BF16)
        w_bc_piece = jnp.pad(w_bcdt, ((0, 0), (0, -columns % 128)))
        u, g, w_x, w_z, w_bc, w_o = gather_plain(u_piece, cotangent, w_zx, w_bc_piece, w_out)
        u = u.reshape(tokens, model)
        g = g.reshape(tokens, model)
        x = dot(u, w_x).reshape(seqs, length, channels)
        z = dot(u, w_z)
        bc_dt = dot(u, w_bc).reshape(seqs, length, -1)
        bc = bc_dt[:, :, :n2]
        dt = jnp.swapaxes(lax.dynamic_slice_in_dim(bc_dt, n2 + tensor * heads, heads, 2), 1, 2)
        y, cx, cbc, states = ssd_forward(x, bc, dt, marks, shared)
        d_normed = dot_nt(g, w_o)
        sig_z = sigmoid(z)
        silu_z = z * sig_z
        y_flat = y.reshape(tokens, channels)
        gated = y_flat * silu_z
        scaled = d_normed * gate_gain
        sums = jnp.stack([jnp.sum(gated * gated, axis=1), jnp.sum(scaled * gated, axis=1)])
        sums = lax.psum(sums, "tensor") / (channels * n_tensor)
        inverse = lax.rsqrt(sums[0] + EPS)[:, None]
        normed = (gated * inverse * gate_gain).astype(BF16)
        grad_gate = jnp.sum(d_normed * gated * inverse, axis=0)[None]
        d_gated = inverse * scaled - gated * inverse**3 * sums[1][:, None]
        dy = (d_gated * silu_z).astype(BF16)
        dz = (d_gated * y_flat * (sig_z * (1.0 + z * (1.0 - sig_z)))).astype(BF16)
        x, bc = x.astype(BF16), bc.astype(BF16)

    back_args = (dy.reshape(seqs, length, channels), x, cx, bc, cbc, dt, marks, states, shared)
    if kernels:
        mixed, grad_out, grad_z, *rest = backward_all(n_dp, w_bc.shape[1], piece, normed, g, u, dz, w_o, *back_args)
    else:
        mixed, grad_out, grad_z = scatter_out_plain(piece, normed, g, u, dz, w_o)
        rest = ssd_backward(w_bc.shape[1], *back_args)
    dx, dbc, gx, gbc, gh = rest
    in_args = (piece, u, dz, dx.reshape(tokens, channels), w_z, w_x, w_bc, dbc.reshape(tokens, -1))
    if kernels:
        d_in, grad_zx, grad_bc, sums, dots, grad_pre = scatter_in(
            n_dp, *in_args, grad_z, gx, gbc, gh, grad_gate, pre_gain[None]
        )
        grad_pre = grad_pre.reshape(model)
        out_hidden, d_hidden, grad_zx, grad_out, grad_bc, grad_conv_x, grad_conv_bc = finish(
            d_in, hidden, cotangent, mixed, scale_in, dots, pre_gain[None], grad_zx, grad_out, grad_bc, sums, columns, n2
        )
    else:
        d_in, grad_x, grad_bc = scatter_in_plain(*in_args)
        grad_zx = jnp.stack([grad_z, grad_x])
        grad_pre = jnp.sum(d_in * x_piece * scale_in, axis=(0, 1))
        dots = scale_in * jnp.sum(d_in * pre_gain * x_piece, axis=-1, keepdims=True)
        steps = jnp.pad(gh[:, :2].T, ((0, 0), (0, channels - heads)))
        sums = lax.psum(jnp.concatenate([gx[:6], grad_gate, steps]), "dp")
        sums = jnp.concatenate([sums[:7], jnp.concatenate([sums[7, :128], sums[8, : channels - 128]])[None]])
        grad_conv_bc, grad_pre = lax.psum((gbc[:5], grad_pre), ("dp", "tensor"))
        grad_conv_x = sums[:5]
        grad_bc = grad_bc[:, :columns]
        out_hidden = (x_piece + mixed).astype(BF16)
        d_hidden = cotangent.astype(F32) + scale_in * (pre_gain * d_in) - x_piece * (scale_in**2 * dots / model)

    return (
        out_hidden,
        d_hidden,
        grad_pre,
        grad_zx,
        grad_bc,
        grad_conv_x,
        grad_conv_bc,
        sums[7, :heads],
        sums[7, 128 : 128 + heads],
        sums[5].reshape(heads, -1).sum(axis=1),
        sums[6],
        grad_out,
    )


def solution(mesh):
    placed = (
        P("dp", "tensor", None),
        P(),
        P(None, "dp", "tensor"),
        P("dp", None),
        P(None, "tensor"),
        P(),
        P("tensor"),
        P("tensor"),
        P("tensor"),
        P("tensor"),
        P("tensor", "dp"),
        P("dp", "tensor", None),
        P("dp", None),
    )
    return jax.shard_map(
        functools.partial(local, mesh.shape["dp"], mesh.shape["tensor"]),
        mesh=mesh,
        in_specs=placed,
        out_specs=(
            P("dp", "tensor", None),
            P("dp", "tensor", None),
            P(),
            P(None, "dp", "tensor"),
            P("dp", None),
            P(None, "tensor"),
            P(),
            P("tensor"),
            P("tensor"),
            P("tensor"),
            P("tensor"),
            P("tensor", "dp"),
        ),
        check_vma=False,
    )
```

profile of v0, /device:TPU:0, one launch (start us, length us, event | category | flops | bytes accessed | tf_op | source)
XLA Modules:
  0.0 389.3 jit_solution(9895940222096556377)
XLA Ops:
  0.6 0.7 broadcast_in_dim.21
  1.4 0.7 broadcast_in_dim_reshape.3.refs_12_.refs_17_
  2.0 0.7 reshape.50
  2.8 0.1 slice.38
  2.8 0.1 copy.32
  2.9 0.1 broadcast_bitcast_fusion
  3.0 0.9 fusion.1
  3.9 0.1 copy.31
  4.0 0.1 broadcast_bitcast_fusion.1
  4.1 0.9 compare_convert_fusion
  5.1 0.7 stack.51.refs_7_.refs_11_
  5.8 1.7 copy.29.refs_3_
  7.6 172.9 %forward_all.1 = (bf16[2048,2048]{1,0:T(8,128)(2,1)}, bf16[2,1024,2048]{2,1,0:T(8,128)(2,1)}, bf16[2048,1024]{1,0:T(8,128)(2,1)}, bf16[2048,1024]{1,0:T(8,128)(2...) custom-call(bf16[2,256,2048]{2,1,0:T(8,128)(2,1)} %hidden_ref.1, ...), custom_call_target="tpu_custom_call" | custom-call | tf_op jit(solution)/shard_map/forward_all/pallas_call | solution.py:898
  180.5 111.3 %backward_all.1 = (bf16[2,256,2048]{2,1,0:T(8,128)(2,1)}, f32[1024,256]{1,0:T(8,128)}, f32[256,1024]{1,0:T(8,128)}, bf16[2,1024,1024]{2,1,0:T(8,128)(2,1)}, bf16...) custom-call(bf16[2048,1024]{1,0:T(8,128)(2,1)} %get-tuple-element.52.refs_0_, ...), custom_call_target="tpu_custom_call" | custom-call | tf_op jit(solution)/shard_map/backward_all/pallas_call | solution.py:1158
  291.9 80.1 %scatter_in.1 = (bf16[2,256,2048]{2,1,0:T(8,128)(2,1)}, f32[2,256,1024]{2,1,0:T(8,128)}, f32[256,384]{1,0:T(8,128)}, f32[16,1024]{1,0:T(8,128)}, f32[2,256,128]{2,1,0:T(8,128)}, /*index=5*/f32[8,256]{1,0:T(8,128)}) custom-call(bf16[2048,2048]{1,0:T(8,128)(2,1)} %get-tuple-element.50.refs_2_.u_hbm, bf16[2048,1024]{1,0:T(8,128)(2,1)} %get-tuple-element.51.refs_3_.dz_hbm, ...), custom_call_target="tpu_custom_call" | custom-call | tf_op jit(solution)/shard_map/scatter_in/pallas_call | solution.py:1471
  371.9 1.2 slice_bitcast_fusion
  373.1 1.3 copy.35
  374.4 1.4 fusion
  375.9 0.1 reshape_squeeze.3
  375.9 0.6 reduce_sum.9
  376.6 10.7 %finish.1 = (bf16[2,256,2048]{2,1,0:T(8,128)(2,1)}, f32[2,256,2048]{2,1,0:T(8,128)}, f32[2,256,1024]{2,1,0:T(8,128)}, f32[1024,256]{1,0:T(8,128)}, f32[256,320]{...) custom-call(bf16[2,256,2048]{2,1,0:T(8,128)(2,1)} %get-tuple-element.72.d_in_ref, bf16[2,256,2048]{2,1,0:T(8,128)(2,1)} %hidden_ref.1, ...), custom_call_target="tpu_custom_call" | custom-call | tf_op jit(solution)/shard_map/finish/pallas_call | solution.py:1540
  387.2 1.9 copy.30
  (11 shorter events, 0.1 us)
where the time goes:
time: 395 us; the launch traced here: 389 us
  Pallas kernels  375 us (95%)
  local copies, waits for them, and re-layouts  10.9 us (3%)
    pallas_call x1, Pallas kernels, forward_all(): pl.pallas_call(functools.partial(all_kernel, n), grid=(3 * n - 1,), in_sp...  173 us
    pallas_call x1, Pallas kernels, backward_all(): pl.pallas_call(functools.partial(back_kernel, n), grid=(n,), in_specs=[an...  111 us
    pallas_call x1, Pallas kernels, scatter_in(): pl.pallas_call(functools.partial(in_kernel, n), in_specs=[anywhere] * 8 +...  80.1 us
    pallas_call x1, Pallas kernels, finish(): pl.pallas_call(finish_kernel, grid=(grid,), in_specs=[piece_rows(model)]...  10.7 us

commit v1 on v0

--- a/solution.py
+++ b/solution.py
@@ -127,6 +127,7 @@
     cols, factors, carry = head_columns(marks_ref[0, 3:4, :], marks_ref[0, 4:5, :], step, cum, cum)
     source = cum - log2_step(step)
     carry_e = jnp.sum(carry * spread_ref[...].astype(F32), axis=0, keepdims=True)
+    skip_e = jnp.sum(turned(skip_ref[...]) * spread_ref[...].astype(F32), axis=0, keepdims=True)
 
     rows = lax.broadcasted_iota(jnp.int32, (q, q), 0)
     places = lax.broadcasted_iota(jnp.int32, (q, q), 1)
@@ -142,7 +143,7 @@
     xf = xb.astype(F32)
     stb = state[...].astype(BF16)
     states_ref[0, 0] = stb
-    y_ref[...] = dot(c_mat, stb) * dot(factors, pick_ref[:, :channels]) + skip_ref[...] * xf
+    y_ref[...] = dot(c_mat, stb) * dot(factors, pick_ref[:, :channels]) + skip_e * xf
     scaled = (xf * dot(factors, pick_ref[:, channels:])).astype(BF16)
     state[...] = carry_e * state[...] + dot(b_turned, scaled)
     for pair in range(heads // 2):
@@ -217,6 +218,7 @@
     source = cum - log2_step(step)
     cols, factors, carry = head_columns(marks_ref[0, 3:4, :], marks_ref[0, 4:5, :], step, cum, source)
     carry_e = jnp.sum(carry * spread_ref[...].astype(F32), axis=0, keepdims=True)
+    skip_e = jnp.sum(turned(skip_ref[...]) * spread_ref[...].astype(F32), axis=0, keepdims=True)
 
     rows = lax.broadcasted_iota(jnp.int32, (q, q), 0)
     places = lax.broadcasted_iota(jnp.int32, (q, q), 1)
@@ -288,7 +290,7 @@
     cx = cx_ref[0]
     sig = sigmoid(cx)
     gx_ref[5:6, :] += jnp.sum(dyf * (cx * sig).astype(BF16).astype(F32), axis=0, keepdims=True)
-    d_cx = (d_in[...] + skip_ref[...] * dyf) * (sig * (1.0 + cx * (1.0 - sig)))
+    d_cx = (d_in[...] + skip_e * dyf) * (sig * (1.0 + cx * (1.0 - sig)))
     dx_ref[0] = conv_back(d_cx, x_ref[0], ds_x, everywhere, taps_x_ref, gx_ref).astype(BF16)
 
     dsb = d_scores[...].astype(BF16)
@@ -355,7 +357,7 @@
         full(5, n2),
         full(1, heads),
         full(1, heads),
-        full(1, channels),
+        full(1, heads),
         full(heads, channels),
         full(128, 2 * channels),
     ]
@@ -677,12 +679,9 @@
         loads[0].wait()
         x_ring.step(0)
         loads[1].wait()
-        columns = wb_own.shape[1]
-        tail = columns // 128 * 128
         mine = span(dp * rows, rows, 16)
-        wb[mine, :tail] = wb_own[:, :tail]
-        wb[mine, tail:] = jnp.zeros((rows, small_cols - tail), BF16)
-        wb[mine, tail:columns] = wb_own[:, tail:]
+        short = jnp.zeros((small_cols - wb_own.shape[0], rows), BF16)
+        wb[mine, :] = jnp.concatenate([wb_own[...], short], axis=0).T
         small.step(0)
         wait(loads[4:first])
         for s in range(seqs):
@@ -758,7 +757,7 @@
             b % blocks, x, bc, dt, marks_ref, *shared, y.at[at_block, :], cx_ref, cbc_ref, states_ref, *scratch
         )
 
-    c = i - (n + 1)
+    slope = wx
 
     def add_shard(k):
         wait(streams(k))
@@ -776,8 +775,18 @@
             def _():
                 dn[:, e] += value
 
-    @pl.when((c >= 0) & (c < n - 2))
-    def _():
+    def gate_block(e, _):
+        part = span(e * BLOCK, BLOCK, BLOCK)
+        zf = dot(u[part, :], wz[...])
+        sig = sigmoid(zf)
+        silu = zf * sig
+        yf = y[part, :]
+        y[part, :] = yf * silu
+        z[part, :] = silu.astype(BF16)
+        slope[part, :] = (yf * (sig + silu * (1.0 - sig))).astype(BF16)
+        return 0
+
+    def shard_step(c, _):
         @pl.when(c == 0)
         def _():
             token_rows.forward(seqs)
@@ -787,37 +796,39 @@
             start(streams(0))
             add_shard(0)
             start(streams(1))
+            keeps[0].wait()
+            x_ring.finish()
 
         @pl.when((c >= 1) & (c <= 4))
         def _():
-            part = span((c - 1) * (seqs * length // 4), seqs * length // 4, 16)
-            z[part, :] = dot(u[part, :], wz[...]).astype(BF16)
+            lax.fori_loop(2 * (c - 1), 2 * c, gate_block, 0)
 
         add_shard(c + 1)
         start(streams(c + 2))
         out_ring.later(c + 2)
-
-        @pl.when(c == n - 3)
-        def _():
-            add_shard(n - 1)
-            keeps[4].start()
-
-            def block_sums(e, _):
-                part = span(e * BLOCK, BLOCK, BLOCK)
-                zf = z[part, :].astype(F32)
-                gated = y[part, :] * (zf * sigmoid(zf))
-                squares = jnp.sum(gated * gated, axis=1, keepdims=True)
-                inner = jnp.sum(gate_ref[...] * dn[part, :] * gated, axis=1, keepdims=True)
-                lane = lax.broadcasted_iota(jnp.int32, (1, 128), 1)
-                both = jnp.where(lane == 0, squares, jnp.where(lane == 1, inner, 0.0))
-                sums[me, :, part] = both.T[0:8, :]
-                return 0
-
-            lax.fori_loop(0, n, block_sums, 0)
-            for kind in range(3):
-                sums_copy(kind).start()
-
-    e = i - (2 * n - 1)
+        return 0
+
+    @pl.when(i == n + 1)
+    def _():
+        lax.fori_loop(0, n - 2, shard_step, 0)
+        add_shard(n - 1)
+        keeps[4].start()
+
+        def block_sums(e, _):
+            part = span(e * BLOCK, BLOCK, BLOCK)
+            gated = y[part, :]
+            squares = jnp.sum(gated * gated, axis=1, keepdims=True)
+            inner = jnp.sum(gate_ref[...] * dn[part, :] * gated, axis=1, keepdims=True)
+            lane = lax.broadcasted_iota(jnp.int32, (1, 128), 1)
+            both = jnp.where(lane == 0, squares, jnp.where(lane == 1, inner, 0.0))
+            sums[me, :, part] = both.T[0:8, :]
+            return 0
+
+        lax.fori_loop(0, n, block_sums, 0)
+        for kind in range(3):
+            sums_copy(kind).start()
+
+    e = i - (n + 2)
 
     @pl.when(e >= 0)
     def _():
@@ -831,24 +842,20 @@
         whole = (sums[0, :, part] + sums[1, :, part]) + (sums[2, :, part] + sums[3, :, part])
         cols = jnp.concatenate([whole, jnp.zeros((120, BLOCK), F32)], axis=0).T / (4 * width)
         inverse = lax.rsqrt(cols[:, 0:1] + EPS)
-        zf = z[part, :].astype(F32)
-        sig = sigmoid(zf)
-        silu = zf * sig
-        yf = y[part, :]
         dnf = dn[part, :]
         gain = gate_ref[...]
-        gated = yf * silu
+        gated = y[part, :]
         scaled_gated = gated * inverse
         normed_ref[...] = (scaled_gated * gain).astype(BF16)
         grad_ref[...] += jnp.sum(dnf * scaled_gated, axis=0, keepdims=True)
         d_gated = inverse * (dnf * gain) - gated * (inverse * inverse * inverse * cols[:, 1:2])
-        dy_ref[...] = (d_gated * silu).astype(BF16)
-        dz_ref[...] = (d_gated * yf * (sig * (1.0 + zf * (1.0 - sig)))).astype(BF16)
+        dy_ref[...] = (d_gated * z[part, :].astype(F32)).astype(BF16)
+        dz_ref[...] = (d_gated * slope[part, :].astype(F32)).astype(BF16)
 
         @pl.when(e == n - 1)
         def _():
-            wait(keeps)
-            for ring in (x_ring, small, z_ring, out_ring):
+            wait(keeps[1:])
+            for ring in (small, z_ring, out_ring):
                 ring.finish()
             token_rows.finish(2 * seqs)
             for ahead in range(1, n):
@@ -866,14 +873,14 @@
     blocks = length // BLOCK
     n2 = shared[1].shape[1]
     heads = shared[2].shape[1]
-    columns = w_bc.shape[1]
+    columns = w_bc.shape[0]
     small = columns + -columns % 128
     sem = pltpu.SemaphoreType.DMA
     ring = [sem((2, 2, n - 1))] * 2
     anywhere = pl.BlockSpec(memory_space=pl.ANY)
     whole = lambda *shape: pl.BlockSpec(shape, lambda i: (0,) * len(shape))
     b = lambda i: jnp.minimum(jnp.maximum(i - 1, 0), n - 1)
-    e = lambda i: jnp.maximum(i - (2 * n - 1), 0)
+    e = lambda i: jnp.maximum(i - (n + 2), 0)
     tok = lambda w: pl.BlockSpec((1, BLOCK, w), lambda i: (b(i) // blocks, b(i) % blocks, 0))
     gate = pl.BlockSpec((BLOCK, width), lambda i: (e(i), 0))
     out_shape = [
@@ -897,7 +904,7 @@
     ]
     return pl.pallas_call(
         functools.partial(all_kernel, n),
-        grid=(3 * n - 1,),
+        grid=(2 * n + 2,),
         in_specs=[anywhere] * 5
         + [
             whole(1, model),
@@ -1522,7 +1529,7 @@
     out_ref[0] = (x + mixed_ref[0].astype(F32)).astype(BF16)
     gzx_ref[...] = gzx_in[...]
     gout_ref[...] = gout_in[...]
-    gb_ref[...] = gb_in[:, : gb_ref.shape[1]]
+    gb_ref[...] = gb_in[...].T[: gb_ref.shape[0], :]
     taps_ref[...] = sums_ref[0 : taps_ref.shape[0], :]
     taps_bc_ref[...] = sums_ref[8 : 8 + taps_bc_ref.shape[0], : taps_bc_ref.shape[1]]
 
@@ -1530,7 +1537,7 @@
 def finish(d_in, hidden, cotangent, mixed, scale, dots, gain, grad_zx, grad_out, grad_bc, sums, columns, n2):
     seqs, piece, model = hidden.shape
     count, width = grad_zx.shape[1:]
-    steps = 4
+    steps = 2
     rows = piece // steps
     grid = seqs * steps
     piece_rows = lambda w: pl.BlockSpec((1, rows, w), lambda i: (i // steps, i % steps, 0))
@@ -1542,16 +1549,16 @@
         grid=(grid,),
         in_specs=[piece_rows(model)] * 4
         + [piece_rows(128)] * 2
-        + [whole(1, model), zx, down(grad_out, grad_out.shape[1]), down(grad_bc, grad_bc.shape[1])]
+        + [whole(1, model), zx, down(grad_out, grad_out.shape[1]), whole(*grad_bc.shape)]
         + [whole(*sums.shape)],
         out_specs=[piece_rows(model)] * 2
-        + [zx, down(grad_out, grad_out.shape[1]), down(grad_bc, columns), whole(5, width), whole(5, n2)],
+        + [zx, down(grad_out, grad_out.shape[1]), whole(columns, count), whole(5, width), whole(5, n2)],
         out_shape=[
             jax.ShapeDtypeStruct(hidden.shape, BF16),
             jax.ShapeDtypeStruct(hidden.shape, F32),
             jax.ShapeDtypeStruct(grad_zx.shape, F32),
             jax.ShapeDtypeStruct(grad_out.shape, F32),
-            jax.ShapeDtypeStruct((grad_bc.shape[0], columns), F32),
+            jax.ShapeDtypeStruct((columns, count), F32),
             jax.ShapeDtypeStruct((5, width), F32),
             jax.ShapeDtypeStruct((5, n2), F32),
         ],
@@ -1632,12 +1639,11 @@
     x_piece = hidden.astype(F32)
     marks = row_marks(segments)
     spread = jnp.asarray(spread_matrix(heads, channels), BF16)
-    skip = jnp.repeat(d_skip, channels // heads)[None]
     pick = jnp.asarray(pick_matrix(heads, channels), BF16)
-    shared = (conv_x, conv_bc, dt_bias[None], a_log[None], skip, spread, pick)
+    shared = (conv_x, conv_bc, dt_bias[None], a_log[None], d_skip[None], spread, pick)
     if kernels:
         u, g, w_x, w_z, w_bc, w_o, cx, x, cbc, bc, dt, states, normed, dz, dy, grad_gate, scale_in = forward_all(
-            n_dp, hidden, cotangent, w_zx, w_bcdt, w_out, pre_gain[None], gate_gain[None], marks, shared
+            n_dp, hidden, cotangent, w_zx, w_bcdt.T, w_out, pre_gain[None], gate_gain[None], marks, shared
         )
         g = g.reshape(tokens, model)
     else:
@@ -1685,6 +1691,7 @@
         out_hidden, d_hidden, grad_zx, grad_out, grad_bc, grad_conv_x, grad_conv_bc = finish(
             d_in, hidden, cotangent, mixed, scale_in, dots, pre_gain[None], grad_zx, grad_out, grad_bc, sums, columns, n2
         )
+        grad_bc = grad_bc.T
     else:
         d_in, grad_x, grad_bc = scatter_in_plain(*in_args)
         grad_zx = jnp.stack([grad_z, grad_x])

time: 395 us -> 384 us (0.972)
  Pallas kernels: 375 us -> 370 us
  local copies, waits for them, and re-layouts: 10.9 us -> 5.94 us
    pallas_call x1, Pallas kernels: 173 us -> 168 us  [forward_all(): pl.pallas_call(functools.partial(all_kernel, n), grid=(2 * n + 2,), in_sp...]
where the time goes in v1:
time: 384 us; the launch traced here: 380 us
  Pallas kernels  370 us (96%)
  local copies, waits for them, and re-layouts  5.94 us (2%)
    pallas_call x1, Pallas kernels, forward_all(): pl.pallas_call(functools.partial(all_kernel, n), grid=(2 * n + 2,), in_sp...  168 us
    pallas_call x1, Pallas kernels, backward_all(): pl.pallas_call(functools.partial(back_kernel, n), grid=(n,), in_specs=[an...  112 us
    pallas_call x1, Pallas kernels, scatter_in(): pl.pallas_call(functools.partial(in_kernel, n), in_specs=[anywhere] * 8 +...  80.3 us
    pallas_call x1, Pallas kernels, finish(): pl.pallas_call(finish_kernel, grid=(grid,), in_specs=[piece_rows(model)]...  9.11 us

profile of v1, /device:TPU:0, one launch (start us, length us, event | category | flops | bytes accessed | tf_op | source)
XLA Modules:
  0.0 379.5 jit_solution(12723707716547244538)
XLA Ops:
  0.6 0.7 reshape.50
  1.4 0.1 slice.38
  1.4 0.1 copy.30
  1.5 0.1 broadcast_bitcast_fusion
  1.6 0.9 fusion.1
  2.5 0.1 copy.29
  2.6 0.1 broadcast_bitcast_fusion.1
  2.7 0.9 compare_convert_fusion
  3.7 0.7 stack.51.refs_7_.refs_11_
  4.4 168.3 %forward_all.1 = (bf16[2048,2048]{1,0:T(8,128)(2,1)}, bf16[2,1024,2048]{2,1,0:T(8,128)(2,1)}, bf16[2048,1024]{1,0:T(8,128)(2,1)}, bf16[2048,1024]{1,0:T(8,128)(2...) custom-call(bf16[2,256,2048]{2,1,0:T(8,128)(2,1)} %hidden_ref.1, ...), custom_call_target="tpu_custom_call" | custom-call | tf_op jit(solution)/shard_map/forward_all/pallas_call | solution.py:905
  172.8 112.5 %backward_all.1 = (bf16[2,256,2048]{2,1,0:T(8,128)(2,1)}, f32[1024,256]{1,0:T(8,128)}, f32[256,1024]{1,0:T(8,128)}, bf16[2,1024,1024]{2,1,0:T(8,128)(2,1)}, bf16...) custom-call(bf16[2048,1024]{1,0:T(8,128)(2,1)} %get-tuple-element.52.refs_0_, ...), custom_call_target="tpu_custom_call" | custom-call | tf_op jit(solution)/shard_map/backward_all/pallas_call | solution.py:1165
  285.3 80.3 %scatter_in.1 = (bf16[2,256,2048]{2,1,0:T(8,128)(2,1)}, f32[2,256,1024]{2,1,0:T(8,128)}, f32[256,384]{1,0:T(8,128)}, f32[16,1024]{1,0:T(8,128)}, f32[2,256,128]{2,1,0:T(8,128)}, /*index=5*/f32[8,256]{1,0:T(8,128)}) custom-call(bf16[2048,2048]{1,0:T(8,128)(2,1)} %get-tuple-element.50.refs_2_.u_hbm, bf16[2048,1024]{1,0:T(8,128)(2,1)} %get-tuple-element.51.refs_3_.dz_hbm, ...), custom_call_target="tpu_custom_call" | custom-call | tf_op jit(solution)/shard_map/scatter_in/pallas_call | solution.py:1478
  365.6 1.2 slice_bitcast_fusion
  366.8 1.3 copy.33
  368.1 1.4 fusion
  369.5 0.1 reshape_squeeze.3
  369.6 0.6 reduce_sum.9
  370.2 9.1 %finish.1 = (bf16[2,256,2048]{2,1,0:T(8,128)(2,1)}, f32[2,256,2048]{2,1,0:T(8,128)}, f32[2,256,1024]{2,1,0:T(8,128)}, f32[1024,256]{1,0:T(8,128)}, f32[320,256]{...) custom-call(bf16[2,256,2048]{2,1,0:T(8,128)(2,1)} %get-tuple-element.72.d_in_ref, bf16[2,256,2048]{2,1,0:T(8,128)(2,1)} %hidden_ref.1, ...), custom_call_target="tpu_custom_call" | custom-call | tf_op jit(solution)/shard_map/finish/pallas_call | solution.py:1547
  (11 shorter events, 0.1 us)

commit v2 on v1

--- a/solution.py
+++ b/solution.py
@@ -568,12 +568,27 @@
                 self.copy(kind, part).wait_send()
 
 
+def marks_of(seg):
+    length = seg.shape[1]
+    lane = lax.broadcasted_iota(jnp.int32, seg.shape, 1)
+    row = lax.broadcasted_iota(jnp.int32, seg.shape, 0)
+    earlier = [jnp.where(lane < lag, -1.0, pltpu.roll(seg, lag, 1)) for lag in (1, 2, 3)]
+    starts = range(0, length, BLOCK)
+    spread = lambda values, at: jnp.broadcast_to(values[:, at : at + 1], (seg.shape[0], BLOCK))
+    before = jnp.concatenate([spread(earlier[0], at) for at in starts], axis=1)
+    final = jnp.concatenate([spread(seg, at + BLOCK - 1) for at in starts], axis=1)
+    out = jnp.where(row == 5, seg, 0.0)
+    for k, other in enumerate((*earlier, before, final)):
+        out = jnp.where((row == k) & (other == seg), 1.0, out)
+    return out
+
+
 def all_kernel(n, *refs):
-    (hidden_ref, g_ref, wzx_ref, wbc_ref, wout_ref, gain_ref, gate_ref, marks_ref), refs = refs[:8], refs[8:]
+    (hidden_ref, g_ref, wzx_ref, wbc_ref, wout_ref, gain_ref, gate_ref, seg_ref), refs = refs[:8], refs[8:]
     shared, refs = refs[:7], refs[7:]
     (u_out, gf_out, wx_out, wz_out, wb_out, wo_out), refs = refs[:6], refs[6:]
     (cx_ref, x_ref, cbc_ref, bc_ref, dt_ref, states_ref), refs = refs[:6], refs[6:]
-    (normed_ref, dz_ref, dy_ref, grad_ref, scale_ref), refs = refs[:5], refs[5:]
+    (normed_ref, dz_ref, dy_ref, grad_ref, scale_ref, marks_ref), refs = refs[:6], refs[6:]
     scratch, refs = refs[:4], refs[4:]
     (u, wx, wz, wo, wb, wb_own, wdt, g_cols, y, z, dn, sums), refs = refs[:12], refs[12:]
     (load_sem, keep_sem, stream_sem), sems = refs[:3], refs[3:]
@@ -694,6 +709,9 @@
             u[to, cut(0)] = (left * scale * gain_ref[:, cut(0)]).astype(BF16)
             u[to, cut(1)] = (right * scale * gain_ref[:, cut(1)]).astype(BF16)
             token_rows.start(s)
+        for s in range(seqs):
+            seg = seg_ref[s : s + 1, :].astype(F32)
+            marks_ref[s] = marks_of(jnp.broadcast_to(seg, (8, seg.shape[1])))
         wait(loads[first:])
         start(stores)
         wait(loads[2:4])
@@ -747,6 +765,7 @@
 
         at_block = span(b * BLOCK, BLOCK, BLOCK)
         tokens = u[at_block, :]
+        marks = marks_ref.at[pl.ds(b // blocks, 1), :, span(b % blocks * BLOCK, BLOCK, BLOCK)]
         x = dot(tokens, wx[...])
         bc = dot(tokens, wb[:, :n2])
         dt = dot_nt(wdt[...], tokens)
@@ -754,7 +773,7 @@
         bc_ref[0] = bc.astype(BF16)
         dt_ref[0] = dt
         forward_block(
-            b % blocks, x, bc, dt, marks_ref, *shared, y.at[at_block, :], cx_ref, cbc_ref, states_ref, *scratch
+            b % blocks, x, bc, dt, marks, *shared, y.at[at_block, :], cx_ref, cbc_ref, states_ref, *scratch
         )
 
     slope = wx
@@ -864,7 +883,7 @@
                 sums_copy(kind).wait_send()
 
 
-def forward_all(n, hidden, g, w_zx, w_bc, w_out, pre_gain, gate_gain, marks, shared):
+def forward_all(n, hidden, g, w_zx, w_bc, w_out, pre_gain, gate_gain, segments, shared):
     seqs, piece, model = hidden.shape
     rows, width = w_zx.shape[1:]
     out_rows, out_cols = w_out.shape
@@ -901,6 +920,7 @@
         ((tokens, width), BF16),
         ((1, width), F32),
         ((seqs, piece, 128), F32),
+        ((seqs, 8, length), F32),
     ]
     return pl.pallas_call(
         functools.partial(all_kernel, n),
@@ -909,7 +929,7 @@
         + [
             whole(1, model),
             whole(1, width),
-            pl.BlockSpec((1, 8, BLOCK), lambda i: (b(i) // blocks, 0, b(i) % blocks)),
+            whole(*segments.shape),
         ]
         + shared_specs(width, n2, heads),
         out_specs=[anywhere] * 6
@@ -917,7 +937,7 @@
         + [pl.BlockSpec((1, heads, BLOCK), lambda i: (b(i) // blocks, 0, b(i) % blocks))]
         + [pl.BlockSpec((1, 1, n2 // 2, width), lambda i: (b(i) // blocks, b(i) % blocks, 0, 0))]
         + [gate] * 3
-        + [whole(1, width), whole(seqs, piece, 128)],
+        + [whole(1, width), whole(seqs, piece, 128), whole(seqs, 8, length)],
         out_shape=[jax.ShapeDtypeStruct(*s) for s in out_shape],
         scratch_shapes=forward_scratch(width, n2)
         + [
@@ -943,7 +963,7 @@
             collective_id=0, has_side_effects=True, vmem_limit_bytes=63 * 2**20
         ),
         name="forward_all",
-    )(hidden, g, w_zx, w_bc, w_out, pre_gain, gate_gain, marks, *shared)
+    )(hidden, g, w_zx, w_bc, w_out, pre_gain, gate_gain, segments, *shared)
 
 
 class RingScatter:
@@ -1637,13 +1657,12 @@
     kernels = n_dp == 8 and n_tensor == 4 and seqs == 2 and length == 4 * BLOCK
 
     x_piece = hidden.astype(F32)
-    marks = row_marks(segments)
     spread = jnp.asarray(spread_matrix(heads, channels), BF16)
     pick = jnp.asarray(pick_matrix(heads, channels), BF16)
     shared = (conv_x, conv_bc, dt_bias[None], a_log[None], d_skip[None], spread, pick)
     if kernels:
-        u, g, w_x, w_z, w_bc, w_o, cx, x, cbc, bc, dt, states, normed, dz, dy, grad_gate, scale_in = forward_all(
-            n_dp, hidden, cotangent, w_zx, w_bcdt.T, w_out, pre_gain[None], gate_gain[None], marks, shared
+        u, g, w_x, w_z, w_bc, w_o, cx, x, cbc, bc, dt, states, normed, dz, dy, grad_gate, scale_in, marks = forward_all(
+            n_dp, hidden, cotangent, w_zx, w_bcdt.T, w_out, pre_gain[None], gate_gain[None], segments, shared
         )
         g = g.reshape(tokens, model)
     else:
@@ -1658,6 +1677,7 @@
         bc_dt = dot(u, w_bc).reshape(seqs, length, -1)
         bc = bc_dt[:, :, :n2]
         dt = jnp.swapaxes(lax.dynamic_slice_in_dim(bc_dt, n2 + tensor * heads, heads, 2), 1, 2)
+        marks = row_marks(segments)
         y, cx, cbc, states = ssd_forward(x, bc, dt, marks, shared)
         d_normed = dot_nt(g, w_o)
         sig_z = sigmoid(z)

time: 384 us -> 380 us (0.990)
  no operation moved by 1% of the time
where the time goes in v2:
time: 380 us; the launch traced here: 376 us
  Pallas kernels  370 us (97%)
  local copies, waits for them, and re-layouts  4 us (1%)
    pallas_call x1, Pallas kernels, forward_all(): pl.pallas_call(functools.partial(all_kernel, n), grid=(2 * n + 2,), in_sp...  169 us
    pallas_call x1, Pallas kernels, backward_all(): pl.pallas_call(functools.partial(back_kernel, n), grid=(n,), in_specs=[an...  112 us
    pallas_call x1, Pallas kernels, scatter_in(): pl.pallas_call(functools.partial(in_kernel, n), in_specs=[anywhere] * 8 +...  80.4 us
    pallas_call x1, Pallas kernels, finish(): pl.pallas_call(finish_kernel, grid=(grid,), in_specs=[piece_rows(model)]...  9.11 us

profile of v2, /device:TPU:0, one launch (start us, length us, event | category | flops | bytes accessed | tf_op | source)
XLA Modules:
  0.0 375.9 jit_solution(13699467437549000320)
XLA Ops:
  0.6 168.7 %forward_all.1 = (bf16[2048,2048]{1,0:T(8,128)(2,1)}, bf16[2,1024,2048]{2,1,0:T(8,128)(2,1)}, bf16[2048,1024]{1,0:T(8,128)(2,1)}, bf16[2048,1024]{1,0:T(8,128)(2...) custom-call(bf16[2,256,2048]{2,1,0:T(8,128)(2,1)} %hidden_ref.1, ...), custom_call_target="tpu_custom_call" | custom-call | tf_op jit(solution)/shard_map/forward_all/pallas_call | solution.py:925
  169.3 112.1 %backward_all.1 = (bf16[2,256,2048]{2,1,0:T(8,128)(2,1)}, f32[1024,256]{1,0:T(8,128)}, f32[256,1024]{1,0:T(8,128)}, bf16[2,1024,1024]{2,1,0:T(8,128)(2,1)}, bf16...) custom-call(bf16[2048,1024]{1,0:T(8,128)(2,1)} %get-tuple-element.53.refs_0_, ...), custom_call_target="tpu_custom_call" | custom-call | tf_op jit(solution)/shard_map/backward_all/pallas_call | solution.py:1185
  281.5 80.4 %scatter_in.1 = (bf16[2,256,2048]{2,1,0:T(8,128)(2,1)}, f32[2,256,1024]{2,1,0:T(8,128)}, f32[256,384]{1,0:T(8,128)}, f32[16,1024]{1,0:T(8,128)}, f32[2,256,128]{2,1,0:T(8,128)}, /*index=5*/f32[8,256]{1,0:T(8,128)}) custom-call(bf16[2048,2048]{1,0:T(8,128)(2,1)} %get-tuple-element.51.refs_2_.u_hbm, bf16[2048,1024]{1,0:T(8,128)(2,1)} %get-tuple-element.52.refs_3_.dz_hbm, ...), custom_call_target="tpu_custom_call" | custom-call | tf_op jit(solution)/shard_map/scatter_in/pallas_call | solution.py:1498
  361.9 1.2 slice_bitcast_fusion
  363.1 1.3 copy.27
  364.4 1.4 fusion
  365.8 0.1 reshape_squeeze.3
  365.9 0.6 reduce_sum.9
  366.5 9.1 %finish.1 = (bf16[2,256,2048]{2,1,0:T(8,128)(2,1)}, f32[2,256,2048]{2,1,0:T(8,128)}, f32[2,256,1024]{2,1,0:T(8,128)}, f32[1024,256]{1,0:T(8,128)}, f32[320,256]{...) custom-call(bf16[2,256,2048]{2,1,0:T(8,128)(2,1)} %get-tuple-element.74.d_in_ref, bf16[2,256,2048]{2,1,0:T(8,128)(2,1)} %hidden_ref.1, ...), custom_call_target="tpu_custom_call" | custom-call | tf_op jit(solution)/shard_map/finish/pallas_call | solution.py:1567

commit v3 on v2

--- a/solution.py
+++ b/solution.py
@@ -1539,7 +1539,9 @@
 
 def finish_kernel(
     d_in_ref, hidden_ref, cot_ref, mixed_ref, scale_ref, dots_ref, gain_ref, gzx_in, gout_in, gb_in, sums_ref,
+    spread_ref, pre_in,
     out_ref, d_hidden_ref, gzx_ref, gout_ref, gb_ref, taps_ref, taps_bc_ref,
+    bias_ref, alog_ref, skip_ref, gate_ref, pre_ref,
 ):
     model = gain_ref.shape[1]
     x = hidden_ref[0].astype(F32)
@@ -1552,11 +1554,29 @@
     gb_ref[...] = gb_in[...].T[: gb_ref.shape[0], :]
     taps_ref[...] = sums_ref[0 : taps_ref.shape[0], :]
     taps_bc_ref[...] = sums_ref[8 : 8 + taps_bc_ref.shape[0], : taps_bc_ref.shape[1]]
-
-
-def finish(d_in, hidden, cotangent, mixed, scale, dots, gain, grad_zx, grad_out, grad_bc, sums, columns, n2):
+    heads = bias_ref.shape[0]
+    bias_ref[...] = sums_ref[7, 0:heads]
+    alog_ref[...] = sums_ref[7, 128 : 128 + heads]
+    gate_ref[...] = sums_ref[6, :]
+    by_head = lax.dot_general(
+        sums_ref[0:8, :],
+        spread_ref[...].astype(F32),
+        (((1,), (1,)), ((), ())),
+        precision=EXACT,
+        preferred_element_type=F32,
+    )
+    skip_ref[...] = by_head[5, :]
+    wide = pre_in.shape[1]
+    for i in range(pre_in.shape[0]):
+        pre_ref[pl.ds(i * wide, wide)] = pre_in[i, :]
+
+
+def finish(
+    d_in, hidden, cotangent, mixed, scale, dots, gain, grad_zx, grad_out, grad_bc, sums, spread, pre, columns, n2
+):
     seqs, piece, model = hidden.shape
     count, width = grad_zx.shape[1:]
+    heads = spread.shape[0]
     steps = 2
     rows = piece // steps
     grid = seqs * steps
@@ -1570,9 +1590,10 @@
         in_specs=[piece_rows(model)] * 4
         + [piece_rows(128)] * 2
         + [whole(1, model), zx, down(grad_out, grad_out.shape[1]), whole(*grad_bc.shape)]
-        + [whole(*sums.shape)],
+        + [whole(*sums.shape), whole(*spread.shape), whole(*pre.shape)],
         out_specs=[piece_rows(model)] * 2
-        + [zx, down(grad_out, grad_out.shape[1]), whole(columns, count), whole(5, width), whole(5, n2)],
+        + [zx, down(grad_out, grad_out.shape[1]), whole(columns, count), whole(5, width), whole(5, n2)]
+        + [whole(heads), whole(heads), whole(heads), whole(width), whole(model)],
         out_shape=[
             jax.ShapeDtypeStruct(hidden.shape, BF16),
             jax.ShapeDtypeStruct(hidden.shape, F32),
@@ -1581,10 +1602,11 @@
             jax.ShapeDtypeStruct((columns, count), F32),
             jax.ShapeDtypeStruct((5, width), F32),
             jax.ShapeDtypeStruct((5, n2), F32),
-        ],
+        ]
+        + [jax.ShapeDtypeStruct((k,), F32) for k in (heads, heads, heads, width, model)],
         compiler_params=pltpu.CompilerParams(vmem_limit_bytes=62 * 2**20),
         name="finish",
-    )(d_in, hidden, cotangent, mixed, scale, dots, gain, grad_zx, grad_out, grad_bc, sums)
+    )(d_in, hidden, cotangent, mixed, scale, dots, gain, grad_zx, grad_out, grad_bc, sums, spread, pre)
 
 
 def rms_scale(values):
@@ -1707,10 +1729,12 @@
         d_in, grad_zx, grad_bc, sums, dots, grad_pre = scatter_in(
             n_dp, *in_args, grad_z, gx, gbc, gh, grad_gate, pre_gain[None]
         )
-        grad_pre = grad_pre.reshape(model)
-        out_hidden, d_hidden, grad_zx, grad_out, grad_bc, grad_conv_x, grad_conv_bc = finish(
-            d_in, hidden, cotangent, mixed, scale_in, dots, pre_gain[None], grad_zx, grad_out, grad_bc, sums, columns, n2
+        finished = finish(
+            d_in, hidden, cotangent, mixed, scale_in, dots, pre_gain[None], grad_zx, grad_out, grad_bc, sums, spread,
+            grad_pre, columns, n2
         )
+        out_hidden, d_hidden, grad_zx, grad_out, grad_bc, grad_conv_x, grad_conv_bc, *small = finished
+        grad_bias, grad_alog, grad_skip, grad_gate, grad_pre = small
         grad_bc = grad_bc.T
     else:
         d_in, grad_x, grad_bc = scatter_in_plain(*in_args)
@@ -1722,6 +1746,9 @@
         sums = jnp.concatenate([sums[:7], jnp.concatenate([sums[7, :128], sums[8, : channels - 128]])[None]])
         grad_conv_bc, grad_pre = lax.psum((gbc[:5], grad_pre), ("dp", "tensor"))
         grad_conv_x = sums[:5]
+        grad_bias, grad_alog = sums[7, :heads], sums[7, 128 : 128 + heads]
+        grad_skip = sums[5].reshape(heads, -1).sum(axis=1)
+        grad_gate = sums[6]
         grad_bc = grad_bc[:, :columns]
         out_hidden = (x_piece + mixed).astype(BF16)
         d_hidden = cotangent.astype(F32) + scale_in * (pre_gain * d_in) - x_piece * (scale_in**2 * dots / model)
@@ -1734,10 +1761,10 @@
         grad_bc,
         grad_conv_x,
         grad_conv_bc,
-        sums[7, :heads],
-        sums[7, 128 : 128 + heads],
-        sums[5].reshape(heads, -1).sum(axis=1),
-        sums[6],
+        grad_bias,
+        grad_alog,
+        grad_skip,
+        grad_gate,
         grad_out,
     )
 

time: 380 us -> 376 us (0.989)
  local copies, waits for them, and re-layouts: 4 us -> 0 us
where the time goes in v3:
time: 376 us; the launch traced here: 371 us
  Pallas kernels  371 us (99%)
    pallas_call x1, Pallas kernels, forward_all(): pl.pallas_call(functools.partial(all_kernel, n), grid=(2 * n + 2,), in_sp...  169 us
    pallas_call x1, Pallas kernels, backward_all(): pl.pallas_call(functools.partial(back_kernel, n), grid=(n,), in_specs=[an...  112 us
    pallas_call x1, Pallas kernels, scatter_in(): pl.pallas_call(functools.partial(in_kernel, n), in_specs=[anywhere] * 8 +...  80.3 us
    pallas_call x1, Pallas kernels, finish(): pl.pallas_call(finish_kernel, grid=(grid,), in_specs=[piece_rows(model)]...  9.3 us

profile of v3, /device:TPU:0, one launch (start us, length us, event | category | flops | bytes accessed | tf_op | source)
XLA Modules:
  0.0 371.4 jit_solution(11719439967405279173)
XLA Ops:
  0.6 168.8 %forward_all.1 = (bf16[2048,2048]{1,0:T(8,128)(2,1)}, bf16[2,1024,2048]{2,1,0:T(8,128)(2,1)}, bf16[2048,1024]{1,0:T(8,128)(2,1)}, bf16[2048,1024]{1,0:T(8,128)(2...) custom-call(bf16[2,256,2048]{2,1,0:T(8,128)(2,1)} %hidden_ref.1, ...), custom_call_target="tpu_custom_call" | custom-call | tf_op jit(solution)/shard_map/forward_all/pallas_call | solution.py:925
  169.5 112.0 %backward_all.1 = (bf16[2,256,2048]{2,1,0:T(8,128)(2,1)}, f32[1024,256]{1,0:T(8,128)}, f32[256,1024]{1,0:T(8,128)}, bf16[2,1024,1024]{2,1,0:T(8,128)(2,1)}, bf16...) custom-call(bf16[2048,1024]{1,0:T(8,128)(2,1)} %get-tuple-element.58.refs_0_, ...), custom_call_target="tpu_custom_call" | custom-call | tf_op jit(solution)/shard_map/backward_all/pallas_call | solution.py:1185
  281.6 80.3 %scatter_in.1 = (bf16[2,256,2048]{2,1,0:T(8,128)(2,1)}, f32[2,256,1024]{2,1,0:T(8,128)}, f32[256,384]{1,0:T(8,128)}, f32[16,1024]{1,0:T(8,128)}, f32[2,256,128]{2,1,0:T(8,128)}, /*index=5*/f32[8,256]{1,0:T(8,128)}) custom-call(bf16[2048,2048]{1,0:T(8,128)(2,1)} %get-tuple-element.56.refs_2_.u_hbm, bf16[2048,1024]{1,0:T(8,128)(2,1)} %get-tuple-element.57.refs_3_.dz_hbm, ...), custom_call_target="tpu_custom_call" | custom-call | tf_op jit(solution)/shard_map/scatter_in/pallas_call | solution.py:1498
  361.9 9.3 %finish.1 = (bf16[2,256,2048]{2,1,0:T(8,128)(2,1)}, f32[2,256,2048]{2,1,0:T(8,128)}, f32[2,256,1024]{2,1,0:T(8,128)}, f32[1024,256]{1,0:T(8,128)}, f32[320,256]{...) custom-call(bf16[2,256,2048]{2,1,0:T(8,128)(2,1)} %get-tuple-element, ...), custom_call_target="tpu_custom_call" | custom-call | tf_op jit(solution)/shard_map/finish/pallas_call | solution.py:1587

commit v4 on v3

--- a/solution.py
+++ b/solution.py
@@ -747,6 +747,7 @@
         @pl.when(b == n - 2)
         def _():
             out_ring.step(0)
+            token_rows.forward(seqs)
 
         @pl.when(b == n - 1)
         def _():
@@ -776,6 +777,10 @@
             b % blocks, x, bc, dt, marks, *shared, y.at[at_block, :], cx_ref, cbc_ref, states_ref, *scratch
         )
 
+        @pl.when(b == n - 1)
+        def _():
+            token_rows.forward(seqs + 1)
+
     slope = wx
 
     def add_shard(k):
@@ -808,8 +813,6 @@
     def shard_step(c, _):
         @pl.when(c == 0)
         def _():
-            token_rows.forward(seqs)
-            token_rows.forward(seqs + 1)
             token_rows.wait(seqs)
             token_rows.wait(seqs + 1)
             start(streams(0))

time: 376 us -> 377 us (level)
  no operation moved by 1% of the time
where the time goes in v4:
time: 377 us; the launch traced here: 373 us
  Pallas kernels  372 us (99%)
    pallas_call x1, Pallas kernels, forward_all(): pl.pallas_call(functools.partial(all_kernel, n), grid=(2 * n + 2,), in_sp...  169 us
    pallas_call x1, Pallas kernels, backward_all(): pl.pallas_call(functools.partial(back_kernel, n), grid=(n,), in_specs=[an...  113 us
    pallas_call x1, Pallas kernels, scatter_in(): pl.pallas_call(functools.partial(in_kernel, n), in_specs=[anywhere] * 8 +...  80.4 us
    pallas_call x1, Pallas kernels, finish(): pl.pallas_call(finish_kernel, grid=(grid,), in_specs=[piece_rows(model)]...  9.3 us

profile of v4, /device:TPU:0, one launch (start us, length us, event | category | flops | bytes accessed | tf_op | source)
XLA Modules:
  0.0 372.8 jit_solution(4669540613654703371)
XLA Ops:
  0.6 169.2 %forward_all.1 = (bf16[2048,2048]{1,0:T(8,128)(2,1)}, bf16[2,1024,2048]{2,1,0:T(8,128)(2,1)}, bf16[2048,1024]{1,0:T(8,128)(2,1)}, bf16[2048,1024]{1,0:T(8,128)(2...) custom-call(bf16[2,256,2048]{2,1,0:T(8,128)(2,1)} %hidden_ref.1, ...), custom_call_target="tpu_custom_call" | custom-call | tf_op jit(solution)/shard_map/forward_all/pallas_call | solution.py:928
  169.9 113.0 %backward_all.1 = (bf16[2,256,2048]{2,1,0:T(8,128)(2,1)}, f32[1024,256]{1,0:T(8,128)}, f32[256,1024]{1,0:T(8,128)}, bf16[2,1024,1024]{2,1,0:T(8,128)(2,1)}, bf16...) custom-call(bf16[2048,1024]{1,0:T(8,128)(2,1)} %get-tuple-element.58.refs_0_, ...), custom_call_target="tpu_custom_call" | custom-call | tf_op jit(solution)/shard_map/backward_all/pallas_call | solution.py:1188
  282.9 80.4 %scatter_in.1 = (bf16[2,256,2048]{2,1,0:T(8,128)(2,1)}, f32[2,256,1024]{2,1,0:T(8,128)}, f32[256,384]{1,0:T(8,128)}, f32[16,1024]{1,0:T(8,128)}, f32[2,256,128]{2,1,0:T(8,128)}, /*index=5*/f32[8,256]{1,0:T(8,128)}) custom-call(bf16[2048,2048]{1,0:T(8,128)(2,1)} %get-tuple-element.56.refs_2_.u_hbm, bf16[2048,1024]{1,0:T(8,128)(2,1)} %get-tuple-element.57.refs_3_.dz_hbm, ...), custom_call_target="tpu_custom_call" | custom-call | tf_op jit(solution)/shard_map/scatter_in/pallas_call | solution.py:1501
  363.3 9.3 %finish.1 = (bf16[2,256,2048]{2,1,0:T(8,128)(2,1)}, f32[2,256,2048]{2,1,0:T(8,128)}, f32[2,256,1024]{2,1,0:T(8,128)}, f32[1024,256]{1,0:T(8,128)}, f32[320,256]{...) custom-call(bf16[2,256,2048]{2,1,0:T(8,128)(2,1)} %get-tuple-element, ...), custom_call_target="tpu_custom_call" | custom-call | tf_op jit(solution)/shard_map/finish/pallas_call | solution.py:1590
